TPU v7x, 32 devices: a whole 2x2x4 slice. The times are simulated.
32 devices in a mesh: grp: 4 (over y, core), pen: 8 (over z, x).
Axes of the slice: x: 2, y: 2, z: 4, core: 2. Of those that a mesh axis runs over, the one named last changes fastest.
Arguments:
- pressure_source: float32 [16, 1024, 4096], P('grp', None, 'pen'), may hold values from -15 to 15
- solid_temp: float32 [16, 1024, 4096], P(None, 'grp', 'pen'), may hold values from -6 to 6
- gas_wall_temp: float32 [1024, 4096], P('grp', 'pen'), may hold values from -6 to 6
- phase_map: int32 [16, 1024, 4096], P(None, 'grp', 'pen'), may hold values 0 or 1
- phase_conductivity: float32 [2], replicated, may hold values from 0.3 to 1
Outputs:
- pressure: float32 [16, 1024, 4096], P('grp', None, 'pen')
- solid_final: float32 [16, 1024, 4096], P(None, 'grp', 'pen')
All inputs are finite; a program needn't handle non-finite values. No bound on the sum of `phase_map` on one device may be relied on, other than what follows from the above.
Results may differ from a plain program's by a relative error of at most 0.0003.
Values sent between devices are 32-bit elements; how exact they have to be, the bound alone decides.
A program may use at most 128 MiB of HBM per device.

v0:
```python
import math

import jax
import jax.numpy as jnp
from jax import lax
from jax.sharding import PartitionSpec as P

HIGHEST = lax.Precision.HIGHEST
HEAT_TRANSFER = 1.0
PRESSURE_WORK = 0.5
STEP_RATE = 0.12


def broadcast(value, axis, source):
    kept = jnp.where(lax.axis_index(axis) == source, value, 0).astype(value.dtype)
    return lax.psum(kept, axis)


def with_halo(cells, sides, width):
    for axis, dim in sides:
        count = lax.axis_size(axis)
        head = lax.slice_in_dim(cells, 0, width, axis=dim)
        tail = lax.slice_in_dim(cells, cells.shape[dim] - width, cells.shape[dim], axis=dim)
        cells = jnp.concatenate(
            [
                lax.ppermute(tail, axis, [(i, (i + 1) % count) for i in range(count)]),
                cells,
                lax.ppermute(head, axis, [((i + 1) % count, i) for i in range(count)]),
            ],
            axis=dim,
        )
    return cells


def cas_table(row_index, col_index, length):
    product_mod = row_index[:, None] * col_index[None, :] % length
    phase_angle = product_mod.astype(jnp.float32) * (2.0 * math.pi / length)
    return jnp.cos(phase_angle) + jnp.sin(phase_angle)


def depth_solve(source, eigen_sum):
    depth_len = source.shape[0]
    pivot_now = eigen_sum - 1.0
    carry_now = source[0]
    pivot_list = [pivot_now]
    carry_list = [carry_now]
    for plane_idx in range(1, depth_len):
        inverse = 1.0 / pivot_now
        pivot_now = eigen_sum - 2.0 - inverse
        carry_now = source[plane_idx] - inverse * carry_now
        pivot_list.append(pivot_now)
        carry_list.append(carry_now)
    upper_val = carry_list[depth_len - 1] / pivot_list[depth_len - 1]
    result_rows = [upper_val]
    for plane_idx in range(depth_len - 2, -1, -1):
        upper_val = (carry_list[plane_idx] - upper_val) / pivot_list[plane_idx]
        result_rows.append(upper_val)
    return jnp.stack(result_rows[::-1])


def conduct(padded_temp, padded_cond, flux_src):
    centre_temp = padded_temp[:, 1:-1, 1:-1]
    centre_cond = padded_cond[:, 1:-1, 1:-1]
    net_flux = jnp.zeros_like(centre_temp)
    neighbours = (
        (padded_temp[:, :-2, 1:-1], padded_cond[:, :-2, 1:-1]),
        (padded_temp[:, 2:, 1:-1], padded_cond[:, 2:, 1:-1]),
        (padded_temp[:, 1:-1, :-2], padded_cond[:, 1:-1, :-2]),
        (padded_temp[:, 1:-1, 2:], padded_cond[:, 1:-1, 2:]),
    )
    for shift_temp, shift_cond in neighbours:
        net_flux = net_flux + 0.5 * (centre_cond + shift_cond) * (shift_temp - centre_temp)
    vertical = 0.5 * (centre_cond[1:] + centre_cond[:-1]) * (centre_temp[1:] - centre_temp[:-1])
    net_flux = (
        net_flux
        + jnp.pad(vertical, ((0, 1), (0, 0), (0, 0)))
        - jnp.pad(vertical, ((1, 0), (0, 0), (0, 0)))
    )
    surface = jnp.concatenate([flux_src[None], jnp.zeros_like(centre_temp[1:])], axis=0)
    return centre_temp + STEP_RATE * (net_flux + surface)


def per_device(pressure_source, solid_temp, gas_wall_temp, phase_map, phase_conductivity):
    groups = lax.axis_size("grp")
    pencils = lax.axis_size("pen")
    group_idx = lax.axis_index("grp")
    pencil_idx = lax.axis_index("pen")
    depth_loc, span_len, stream_loc = pressure_source.shape
    stream_len = stream_loc * pencils
    depth_len = depth_loc * groups
    span_loc = span_len // (groups * pencils)
    span_index = jnp.arange(span_len, dtype=jnp.int32)
    stream_index = jnp.arange(stream_len, dtype=jnp.int32)
    span_table = cas_table(span_index, span_index, span_len)
    spectral = jnp.einsum(
        "zyx,yw->zwx",
        pressure_source,
        span_table,
        precision=HIGHEST,
        preferred_element_type=jnp.float32,
    )
    moved_data = lax.all_to_all(
        spectral.reshape(1, depth_loc, span_len, stream_loc),
        ("grp", "pen"),
        split_axis=2,
        concat_axis=0,
        tiled=True,
    )
    blocked = moved_data.reshape(groups, pencils, depth_loc, span_loc, stream_loc)
    form_in = "gpzkm,pmw->gzkw"
    block_pens = math.gcd(pencils, max(1, 512 // stream_loc))
    block_cols = stream_loc * block_pens
    block_count = stream_len // block_cols

    def forward_block(block_idx, collected):
        col_index = block_idx * block_cols + jnp.arange(block_cols, dtype=jnp.int32)
        table_part = cas_table(stream_index, col_index, stream_len).reshape(
            pencils, stream_loc, block_cols
        )
        block_out = jnp.einsum(
            form_in, blocked, table_part, precision=HIGHEST, preferred_element_type=jnp.float32
        )
        return lax.dynamic_update_slice_in_dim(collected, block_out, block_idx * block_cols, 3)

    spectrum = lax.fori_loop(
        0,
        block_count,
        forward_block,
        jnp.zeros((groups, depth_loc, span_loc, stream_len), jnp.float32),
    )
    spectrum = spectrum.reshape(depth_len, span_loc, stream_len)
    span_wave = (
        group_idx * (span_len // groups)
        + pencil_idx * span_loc
        + jnp.arange(span_loc, dtype=jnp.int32)
    )
    eigen_span = 2.0 * jnp.cos(span_wave.astype(jnp.float32) * (2.0 * math.pi / span_len)) - 2.0
    eigen_stream = (
        2.0 * jnp.cos(stream_index.astype(jnp.float32) * (2.0 * math.pi / stream_len)) - 2.0
    )
    eigen_sum = eigen_span[:, None] + eigen_stream[None, :]
    solved = depth_solve(spectrum, eigen_sum) * (1.0 / (stream_len * span_len))
    solved_groups = solved.reshape(groups, depth_loc, span_loc, stream_len)

    def backward_block(block_idx, collected):
        col_index = block_idx * block_cols + jnp.arange(block_cols, dtype=jnp.int32)
        table_part = cas_table(stream_index, col_index, stream_len).reshape(
            stream_len, block_pens, stream_loc
        )
        block_out = jnp.einsum(
            "gzkx,xqm->gqzkm",
            solved_groups,
            table_part,
            precision=HIGHEST,
            preferred_element_type=jnp.float32,
        )
        return lax.dynamic_update_slice_in_dim(collected, block_out, block_idx * block_pens, 1)

    physical = lax.fori_loop(
        0,
        block_count,
        backward_block,
        jnp.zeros((groups, pencils, depth_loc, span_loc, stream_loc), jnp.float32),
    )
    returned = lax.all_to_all(
        physical.reshape(groups * pencils, depth_loc, span_loc, stream_loc),
        ("grp", "pen"),
        split_axis=0,
        concat_axis=2,
        tiled=True,
    )
    returned = returned.reshape(depth_loc, span_len, stream_loc)
    inverse_table = cas_table(span_index, span_index, span_len)
    pressure = jnp.einsum(
        "zjx,jy->zyx",
        returned,
        inverse_table,
        precision=HIGHEST,
        preferred_element_type=jnp.float32,
    )
    wall_plane = pressure[0]
    tile_rows = span_len // groups
    whole_plane = broadcast(wall_plane, "grp", 0)
    wall_rows = lax.dynamic_slice_in_dim(whole_plane, group_idx * tile_rows, tile_rows, 0)
    surface_flux = HEAT_TRANSFER * (gas_wall_temp + PRESSURE_WORK * wall_rows - solid_temp[0])
    cell_cond = jnp.where(phase_map == 1, phase_conductivity[1], phase_conductivity[0])
    padded_temp, padded_cond = (
        with_halo(solid_temp, (("grp", 1), ("pen", 2)), 1),
        with_halo(cell_cond, (("grp", 1), ("pen", 2)), 1),
    )
    first_temp = conduct(padded_temp, padded_cond, surface_flux)
    padded_next = with_halo(first_temp, (("grp", 1), ("pen", 2)), 1)
    final_temp = conduct(padded_next, padded_cond, surface_flux)
    return (pressure, final_temp)


def solution(mesh):
    in_specs = (
        P("grp", None, "pen"),
        P(None, "grp", "pen"),
        P("grp", "pen"),
        P(None, "grp", "pen"),
        P(),
    )
    out_specs = (P("grp", None, "pen"), P(None, "grp", "pen"))
    return jax.shard_map(
        per_device, mesh=mesh, in_specs=in_specs, out_specs=out_specs, check_vma=False
    )
```

profile of v0, /device:TPU:0, one launch (start us, length us, event | category | flops | bytes accessed | tf_op | source)
XLA Modules:
  0.0 1537.5 jit_solution(8104873545942355753)
XLA Ops:
  7.2 56.9 %fusion.107 = f32[1,4,1024,512]{3,2,1,0:T(8,128)} fusion(f32[4,1024,512]{2,1,0:T(8,128)} %param.9), kind=kOutput, calls=%fused_computation.145 | convolution fusion | flops 25785532416 | bytes 16777216 | tf_op jit(solution)/shard_map/zyx,yw->zwx/dot_general | solution.py:95
  83.9 185.7 %all-to-all-done = f32[1,4,1024,512]{3,1,0,2:T(4,128)} async-done(((f32[1,4,1024,512]{3,1,0,2:T(4,128)}), f32[1,4,1024,512]{3,1,0,2:T(4,128)}, u32[]{:S(2)}, u32[]{:S(2)}) %all-to-all-start) | async-done | bytes 8388640 | tf_op jit(solution)/shard_map/all_to_all | solution.py:102
  284.4 397.7 %while.32 = (s32[]{:T(128)}, f32[4,4,32,4096]{3,2,1,0:T(8,128)}, f32[4,8,4,32,512]{4,3,1,2,0:T(8,128)}, s32[]{:T(128)}, s32[]{:T(128)}, /*index=5*/s32[]{:T(128)}, s32[]{:T(128)}) while((s32[]{:T(128)}, f32[4,4,32,4096]{3,2,1,0:T(8,128)}, f32[4,8,4,32,512]{4,3,1,2,0:T(8,128)}, s32[]{:T(128)}, s32[]{:T(128)}, /*index=5*/s32[]{:T(128)}, ...), condition=%wide.region_1.2_spmd.clone, body=%wide.region_0.1_spmd.clone.sunk | while | flops 12916368384 | bytes 59805856 | solution.py:125
  284.8 33.1 %fusion.189 = f32[8,512,512,1,1]{2,1,0,4,3:T(8,128)S(1)} fusion(s32[512]{0:T(512)S(1)} %iota_add_fusion.4, s32[8,512]{1,0:T(8,128)S(1)} %multiply_add_fusion.4), kind=kLoop, calls=%fused_computation.11.clone.clone.clone.clone.clone.1.clone.1 | loop fusion | flops 31457280 | bytes 8407040 | tf_op jit(solution)/shard_map/while/body/eval_jaxpr/gpzkm,pmw->gzkw/dot_general | solution.py:120
  317.9 16.5 %fusion.190 = f32[4,4,32,4096]{3,2,1,0:T(8,128)} fusion(f32[4,4,32,4096]{3,2,1,0:T(8,128)} %get-tuple-element.339, s32[]{:T(128)S(6)} %select_n.179, f32[4,8,4,32,512]{4,3,1,2,0:T(8,128)S(1)} %copy-done.1, f32[8,512,512,1,1]{2,1,0,4,3:T(8,128)S(1)} %fusion.189), kind=kOutput, calls=%fused_computation.25.clone.2 | convolution fusion | flops 12884901888 | bytes 17825796 | tf_op jit(solution)/shard_map/while/body/eval_jaxpr/gpzkm,pmw->gzkw/dot_general | solution.py:120
  334.5 33.1 %fusion.189 = f32[8,512,512,1,1]{2,1,0,4,3:T(8,128)S(1)} fusion(s32[512]{0:T(512)S(1)} %iota_add_fusion.4, s32[8,512]{1,0:T(8,128)S(1)} %multiply_add_fusion.4), kind=kLoop, calls=%fused_computation.11.clone.clone.clone.clone.clone.1.clone.1 | loop fusion | flops 31457280 | bytes 8407040 | tf_op jit(solution)/shard_map/while/body/eval_jaxpr/gpzkm,pmw->gzkw/dot_general | solution.py:120
  367.6 16.5 %fusion.190 = f32[4,4,32,4096]{3,2,1,0:T(8,128)} fusion(f32[4,4,32,4096]{3,2,1,0:T(8,128)} %get-tuple-element.339, s32[]{:T(128)S(6)} %select_n.179, f32[4,8,4,32,512]{4,3,1,2,0:T(8,128)S(1)} %copy-done.1, f32[8,512,512,1,1]{2,1,0,4,3:T(8,128)S(1)} %fusion.189), kind=kOutput, calls=%fused_computation.25.clone.2 | convolution fusion | flops 12884901888 | bytes 17825796 | tf_op jit(solution)/shard_map/while/body/eval_jaxpr/gpzkm,pmw->gzkw/dot_general | solution.py:120
  384.1 33.1 %fusion.189 = f32[8,512,512,1,1]{2,1,0,4,3:T(8,128)S(1)} fusion(s32[512]{0:T(512)S(1)} %iota_add_fusion.4, s32[8,512]{1,0:T(8,128)S(1)} %multiply_add_fusion.4), kind=kLoop, calls=%fused_computation.11.clone.clone.clone.clone.clone.1.clone.1 | loop fusion | flops 31457280 | bytes 8407040 | tf_op jit(solution)/shard_map/while/body/eval_jaxpr/gpzkm,pmw->gzkw/dot_general | solution.py:120
  417.2 16.5 %fusion.190 = f32[4,4,32,4096]{3,2,1,0:T(8,128)} fusion(f32[4,4,32,4096]{3,2,1,0:T(8,128)} %get-tuple-element.339, s32[]{:T(128)S(6)} %select_n.179, f32[4,8,4,32,512]{4,3,1,2,0:T(8,128)S(1)} %copy-done.1, f32[8,512,512,1,1]{2,1,0,4,3:T(8,128)S(1)} %fusion.189), kind=kOutput, calls=%fused_computation.25.clone.2 | convolution fusion | flops 12884901888 | bytes 17825796 | tf_op jit(solution)/shard_map/while/body/eval_jaxpr/gpzkm,pmw->gzkw/dot_general | solution.py:120
  433.8 33.1 %fusion.189 = f32[8,512,512,1,1]{2,1,0,4,3:T(8,128)S(1)} fusion(s32[512]{0:T(512)S(1)} %iota_add_fusion.4, s32[8,512]{1,0:T(8,128)S(1)} %multiply_add_fusion.4), kind=kLoop, calls=%fused_computation.11.clone.clone.clone.clone.clone.1.clone.1 | loop fusion | flops 31457280 | bytes 8407040 | tf_op jit(solution)/shard_map/while/body/eval_jaxpr/gpzkm,pmw->gzkw/dot_general | solution.py:120
  466.9 16.5 %fusion.190 = f32[4,4,32,4096]{3,2,1,0:T(8,128)} fusion(f32[4,4,32,4096]{3,2,1,0:T(8,128)} %get-tuple-element.339, s32[]{:T(128)S(6)} %select_n.179, f32[4,8,4,32,512]{4,3,1,2,0:T(8,128)S(1)} %copy-done.1, f32[8,512,512,1,1]{2,1,0,4,3:T(8,128)S(1)} %fusion.189), kind=kOutput, calls=%fused_computation.25.clone.2 | convolution fusion | flops 12884901888 | bytes 17825796 | tf_op jit(solution)/shard_map/while/body/eval_jaxpr/gpzkm,pmw->gzkw/dot_general | solution.py:120
  483.4 33.1 %fusion.189 = f32[8,512,512,1,1]{2,1,0,4,3:T(8,128)S(1)} fusion(s32[512]{0:T(512)S(1)} %iota_add_fusion.4, s32[8,512]{1,0:T(8,128)S(1)} %multiply_add_fusion.4), kind=kLoop, calls=%fused_computation.11.clone.clone.clone.clone.clone.1.clone.1 | loop fusion | flops 31457280 | bytes 8407040 | tf_op jit(solution)/shard_map/while/body/eval_jaxpr/gpzkm,pmw->gzkw/dot_general | solution.py:120
  516.5 16.5 %fusion.190 = f32[4,4,32,4096]{3,2,1,0:T(8,128)} fusion(f32[4,4,32,4096]{3,2,1,0:T(8,128)} %get-tuple-element.339, s32[]{:T(128)S(6)} %select_n.179, f32[4,8,4,32,512]{4,3,1,2,0:T(8,128)S(1)} %copy-done.1, f32[8,512,512,1,1]{2,1,0,4,3:T(8,128)S(1)} %fusion.189), kind=kOutput, calls=%fused_computation.25.clone.2 | convolution fusion | flops 12884901888 | bytes 17825796 | tf_op jit(solution)/shard_map/while/body/eval_jaxpr/gpzkm,pmw->gzkw/dot_general | solution.py:120
  533.0 33.1 %fusion.189 = f32[8,512,512,1,1]{2,1,0,4,3:T(8,128)S(1)} fusion(s32[512]{0:T(512)S(1)} %iota_add_fusion.4, s32[8,512]{1,0:T(8,128)S(1)} %multiply_add_fusion.4), kind=kLoop, calls=%fused_computation.11.clone.clone.clone.clone.clone.1.clone.1 | loop fusion | flops 31457280 | bytes 8407040 | tf_op jit(solution)/shard_map/while/body/eval_jaxpr/gpzkm,pmw->gzkw/dot_general | solution.py:120
  566.1 16.5 %fusion.190 = f32[4,4,32,4096]{3,2,1,0:T(8,128)} fusion(f32[4,4,32,4096]{3,2,1,0:T(8,128)} %get-tuple-element.339, s32[]{:T(128)S(6)} %select_n.179, f32[4,8,4,32,512]{4,3,1,2,0:T(8,128)S(1)} %copy-done.1, f32[8,512,512,1,1]{2,1,0,4,3:T(8,128)S(1)} %fusion.189), kind=kOutput, calls=%fused_computation.25.clone.2 | convolution fusion | flops 12884901888 | bytes 17825796 | tf_op jit(solution)/shard_map/while/body/eval_jaxpr/gpzkm,pmw->gzkw/dot_general | solution.py:120
  582.7 33.1 %fusion.189 = f32[8,512,512,1,1]{2,1,0,4,3:T(8,128)S(1)} fusion(s32[512]{0:T(512)S(1)} %iota_add_fusion.4, s32[8,512]{1,0:T(8,128)S(1)} %multiply_add_fusion.4), kind=kLoop, calls=%fused_computation.11.clone.clone.clone.clone.clone.1.clone.1 | loop fusion | flops 31457280 | bytes 8407040 | tf_op jit(solution)/shard_map/while/body/eval_jaxpr/gpzkm,pmw->gzkw/dot_general | solution.py:120
  632.3 33.1 %fusion.189 = f32[8,512,512,1,1]{2,1,0,4,3:T(8,128)S(1)} fusion(s32[512]{0:T(512)S(1)} %iota_add_fusion.4, s32[8,512]{1,0:T(8,128)S(1)} %multiply_add_fusion.4), kind=kLoop, calls=%fused_computation.11.clone.clone.clone.clone.clone.1.clone.1 | loop fusion | flops 31457280 | bytes 8407040 | tf_op jit(solution)/shard_map/while/body/eval_jaxpr/gpzkm,pmw->gzkw/dot_general | solution.py:120
  701.5 395.6 %while.33 = (s32[]{:T(128)}, f32[4,8,4,32,512]{4,3,2,1,0:T(8,128)}, f32[4,4,32,4096]{3,2,1,0:T(8,128)}, s32[]{:T(128)}, s32[]{:T(128)}) while((s32[]{:T(128)}, f32[4,8,4,32,512]{4,3,2,1,0:T(8,128)}, f32[4,4,32,4096]{3,2,1,0:T(8,128)}, s32[]{:T(128)}, s32[]{:T(128)}) %tuple.109), condition=%wide.region_3.4_spmd.clone, body=%wide.region_2.3_spmd.clone.sunk | while | flops 12916360192 | bytes 59773544 | solution.py:159
  701.8 33.0 %fusion.193 = f32[4096,512,1,1]{1,0,3,2:T(8,128)S(1)} fusion(s32[512]{0:T(512)S(1)} %iota_add_fusion.5), kind=kLoop, calls=%fused_computation.39.clone.clone.clone.clone.clone.1.clone.1 | loop fusion | flops 31457280 | bytes 8390656 | tf_op jit(solution)/shard_map/while/body/eval_jaxpr/gzkx,xqm->gqzkm/dot_general | solution.py:150
  751.1 32.9 %fusion.193 = f32[4096,512,1,1]{1,0,3,2:T(8,128)S(1)} fusion(s32[512]{0:T(512)S(1)} %iota_add_fusion.5), kind=kLoop, calls=%fused_computation.39.clone.clone.clone.clone.clone.1.clone.1 | loop fusion | flops 31457280 | bytes 8390656 | tf_op jit(solution)/shard_map/while/body/eval_jaxpr/gzkx,xqm->gqzkm/dot_general | solution.py:150
  800.5 32.9 %fusion.193 = f32[4096,512,1,1]{1,0,3,2:T(8,128)S(1)} fusion(s32[512]{0:T(512)S(1)} %iota_add_fusion.5), kind=kLoop, calls=%fused_computation.39.clone.clone.clone.clone.clone.1.clone.1 | loop fusion | flops 31457280 | bytes 8390656 | tf_op jit(solution)/shard_map/while/body/eval_jaxpr/gzkx,xqm->gqzkm/dot_general | solution.py:150
  849.9 32.9 %fusion.193 = f32[4096,512,1,1]{1,0,3,2:T(8,128)S(1)} fusion(s32[512]{0:T(512)S(1)} %iota_add_fusion.5), kind=kLoop, calls=%fused_computation.39.clone.clone.clone.clone.clone.1.clone.1 | loop fusion | flops 31457280 | bytes 8390656 | tf_op jit(solution)/shard_map/while/body/eval_jaxpr/gzkx,xqm->gqzkm/dot_general | solution.py:150
  899.2 32.9 %fusion.193 = f32[4096,512,1,1]{1,0,3,2:T(8,128)S(1)} fusion(s32[512]{0:T(512)S(1)} %iota_add_fusion.5), kind=kLoop, calls=%fused_computation.39.clone.clone.clone.clone.clone.1.clone.1 | loop fusion | flops 31457280 | bytes 8390656 | tf_op jit(solution)/shard_map/while/body/eval_jaxpr/gzkx,xqm->gqzkm/dot_general | solution.py:150
  948.6 32.9 %fusion.193 = f32[4096,512,1,1]{1,0,3,2:T(8,128)S(1)} fusion(s32[512]{0:T(512)S(1)} %iota_add_fusion.5), kind=kLoop, calls=%fused_computation.39.clone.clone.clone.clone.clone.1.clone.1 | loop fusion | flops 31457280 | bytes 8390656 | tf_op jit(solution)/shard_map/while/body/eval_jaxpr/gzkx,xqm->gqzkm/dot_general | solution.py:150
  998.0 32.9 %fusion.193 = f32[4096,512,1,1]{1,0,3,2:T(8,128)S(1)} fusion(s32[512]{0:T(512)S(1)} %iota_add_fusion.5), kind=kLoop, calls=%fused_computation.39.clone.clone.clone.clone.clone.1.clone.1 | loop fusion | flops 31457280 | bytes 8390656 | tf_op jit(solution)/shard_map/while/body/eval_jaxpr/gzkx,xqm->gqzkm/dot_general | solution.py:150
  1047.3 32.9 %fusion.193 = f32[4096,512,1,1]{1,0,3,2:T(8,128)S(1)} fusion(s32[512]{0:T(512)S(1)} %iota_add_fusion.5), kind=kLoop, calls=%fused_computation.39.clone.clone.clone.clone.clone.1.clone.1 | loop fusion | flops 31457280 | bytes 8390656 | tf_op jit(solution)/shard_map/while/body/eval_jaxpr/gzkx,xqm->gqzkm/dot_general | solution.py:150
  1119.0 31.7 %collective-permute-done = f32[16,1,512]{2,1,0:T(1,128)S(1)} collective-permute-done((f32[16,1,512]{2,1,0:T(1,128)S(1)}, f32[16,1,512]{2,1,0:T(1,128)S(1)}, u32[]{:S(2)}, u32[]{:S(2)}) %collective-permute-start) | collective-permute-done | bytes 32800 | tf_op jit(solution)/shard_map/ppermute | solution.py:26
  1163.2 126.0 %all-to-all-done.1 = f32[32,4,32,512]{3,2,1,0:T(8,128)} async-done(((f32[32,4,32,512]{3,2,1,0:T(8,128)}), f32[32,4,32,512]{3,2,1,0:T(8,128)}, u32[]{:S(2)}, u32[]{:S(2)}) %all-to-all-start.1) | async-done | bytes 8388640 | tf_op jit(solution)/shard_map/all_to_all | solution.py:165
  1293.7 44.5 %fusion.110 = f32[4,1024,512]{2,1,0:T(8,128)S(1)} fusion(f32[4,1024,512]{2,1,0:T(8,128)S(1)} %bitcast.112), kind=kOutput, calls=%fused_computation.146 | convolution fusion | flops 25785532416 | bytes 16777216 | tf_op jit(solution)/shard_map/zjx,jy->zyx/dot_general | solution.py:174
  1378.6 16.7 %all-reduce.7.cloned.1.call-done = f32[1024,512]{1,0:T(8,128)} async-done(((f32[1024,512]{1,0:T(8,128)}), f32[1024,512]{1,0:T(8,128)}) %all-reduce.7.cloned.1.call-update) | async-done | bytes 2097168 | tf_op jit(solution)/shard_map/psum | solution.py:16
  1396.7 47.3 %fusion.66 = f32[16,256,512]{2,1,0:T(8,128)} fusion(f32[16,256,512]{2,1,0:T(8,128)} %param.10, f32[1,256,512]{2,1,0:T(8,128)S(1)} %fusion.133, f32[16,258,1]{2,1,0:T(8,128)} %copy.40, f32[16,1,512]{2,1,0:T(1,128)S(1)} %collective-permute-done.3, f32[16,1,512]{2,1,0:T(1,128)S(1)} %collective-permute-done.1, f32[16,258,1]{2,1,0:T(8,128)} %copy.36, ...), kind=kLoop, calls=%fused_computation.70 | loop fusion | flops 85983232 | bytes 35848712 | tf_op jit(solution)/shard_map/add | solution.py:80
  1483.1 47.4 %fusion.68 = f32[16,256,512]{2,1,0:T(8,128)} fusion(f32[16,256,512]{2,1,0:T(8,128)} %fusion.66, f32[1,256,512]{2,1,0:T(8,128)S(1)} %fusion.133, f32[16,258,1]{2,1,0:T(8,128)} %copy.44, f32[16,1,512]{2,1,0:T(1,128)S(1)} %collective-permute-done.9, f32[16,1,512]{2,1,0:T(1,128)S(1)} %collective-permute-done.8, f32[16,258,1]{2,1,0:T(8,128)} %copy.42, ...), kind=kLoop, calls=%fused_computation.72 | loop fusion | flops 85983232 | bytes 35848712 | tf_op jit(solution)/shard_map/add | solution.py:80
  (150 shorter events, 337.9 us)
Async XLA Ops:
  76.3 193.3 %all-to-all-start = ((f32[1,4,1024,512]{3,1,0,2:T(4,128)}), f32[1,4,1024,512]{3,1,0,2:T(4,128)}, u32[]{:S(2)}, u32[]{:S(2)}) async-start(f32[1,4,1024,512]{3,1,0,2:T(4,128)} %copy.27), calls=%async_computation | async-start | bytes 16777216 | tf_op jit(solution)/shard_map/all_to_all | solution.py:102
  284.8 33.1 %copy-start.1 = (f32[4,8,4,32,512]{4,3,1,2,0:T(8,128)S(1)}, f32[4,8,4,32,512]{4,3,1,2,0:T(8,128)}, u32[]{:S(2)}) copy-start(f32[4,8,4,32,512]{4,3,1,2,0:T(8,128)} %get-tuple-element.347) | copy-start | bytes 25165828 | tf_op jit(solution)/shard_map/while
  334.5 33.1 %copy-start.1 = (f32[4,8,4,32,512]{4,3,1,2,0:T(8,128)S(1)}, f32[4,8,4,32,512]{4,3,1,2,0:T(8,128)}, u32[]{:S(2)}) copy-start(f32[4,8,4,32,512]{4,3,1,2,0:T(8,128)} %get-tuple-element.347) | copy-start | bytes 25165828 | tf_op jit(solution)/shard_map/while
  384.1 33.1 %copy-start.1 = (f32[4,8,4,32,512]{4,3,1,2,0:T(8,128)S(1)}, f32[4,8,4,32,512]{4,3,1,2,0:T(8,128)}, u32[]{:S(2)}) copy-start(f32[4,8,4,32,512]{4,3,1,2,0:T(8,128)} %get-tuple-element.347) | copy-start | bytes 25165828 | tf_op jit(solution)/shard_map/while
  433.7 33.1 %copy-start.1 = (f32[4,8,4,32,512]{4,3,1,2,0:T(8,128)S(1)}, f32[4,8,4,32,512]{4,3,1,2,0:T(8,128)}, u32[]{:S(2)}) copy-start(f32[4,8,4,32,512]{4,3,1,2,0:T(8,128)} %get-tuple-element.347) | copy-start | bytes 25165828 | tf_op jit(solution)/shard_map/while
  483.4 33.1 %copy-start.1 = (f32[4,8,4,32,512]{4,3,1,2,0:T(8,128)S(1)}, f32[4,8,4,32,512]{4,3,1,2,0:T(8,128)}, u32[]{:S(2)}) copy-start(f32[4,8,4,32,512]{4,3,1,2,0:T(8,128)} %get-tuple-element.347) | copy-start | bytes 25165828 | tf_op jit(solution)/shard_map/while
  533.0 33.1 %copy-start.1 = (f32[4,8,4,32,512]{4,3,1,2,0:T(8,128)S(1)}, f32[4,8,4,32,512]{4,3,1,2,0:T(8,128)}, u32[]{:S(2)}) copy-start(f32[4,8,4,32,512]{4,3,1,2,0:T(8,128)} %get-tuple-element.347) | copy-start | bytes 25165828 | tf_op jit(solution)/shard_map/while
  582.7 33.1 %copy-start.1 = (f32[4,8,4,32,512]{4,3,1,2,0:T(8,128)S(1)}, f32[4,8,4,32,512]{4,3,1,2,0:T(8,128)}, u32[]{:S(2)}) copy-start(f32[4,8,4,32,512]{4,3,1,2,0:T(8,128)} %get-tuple-element.347) | copy-start | bytes 25165828 | tf_op jit(solution)/shard_map/while
  632.3 33.1 %copy-start.1 = (f32[4,8,4,32,512]{4,3,1,2,0:T(8,128)S(1)}, f32[4,8,4,32,512]{4,3,1,2,0:T(8,128)}, u32[]{:S(2)}) copy-start(f32[4,8,4,32,512]{4,3,1,2,0:T(8,128)} %get-tuple-element.347) | copy-start | bytes 25165828 | tf_op jit(solution)/shard_map/while
  701.7 33.0 %copy-start.2 = (f32[4,4,32,4096]{3,2,1,0:T(8,128)S(1)}, f32[4,4,32,4096]{3,2,1,0:T(8,128)}, u32[]{:S(2)}) copy-start(f32[4,4,32,4096]{3,2,1,0:T(8,128)} %get-tuple-element.364) | copy-start | bytes 25165828 | tf_op jit(solution)/shard_map/while
  751.1 33.0 %copy-start.2 = (f32[4,4,32,4096]{3,2,1,0:T(8,128)S(1)}, f32[4,4,32,4096]{3,2,1,0:T(8,128)}, u32[]{:S(2)}) copy-start(f32[4,4,32,4096]{3,2,1,0:T(8,128)} %get-tuple-element.364) | copy-start | bytes 25165828 | tf_op jit(solution)/shard_map/while
  800.5 33.0 %copy-start.2 = (f32[4,4,32,4096]{3,2,1,0:T(8,128)S(1)}, f32[4,4,32,4096]{3,2,1,0:T(8,128)}, u32[]{:S(2)}) copy-start(f32[4,4,32,4096]{3,2,1,0:T(8,128)} %get-tuple-element.364) | copy-start | bytes 25165828 | tf_op jit(solution)/shard_map/while
  849.9 33.0 %copy-start.2 = (f32[4,4,32,4096]{3,2,1,0:T(8,128)S(1)}, f32[4,4,32,4096]{3,2,1,0:T(8,128)}, u32[]{:S(2)}) copy-start(f32[4,4,32,4096]{3,2,1,0:T(8,128)} %get-tuple-element.364) | copy-start | bytes 25165828 | tf_op jit(solution)/shard_map/while
  899.2 33.0 %copy-start.2 = (f32[4,4,32,4096]{3,2,1,0:T(8,128)S(1)}, f32[4,4,32,4096]{3,2,1,0:T(8,128)}, u32[]{:S(2)}) copy-start(f32[4,4,32,4096]{3,2,1,0:T(8,128)} %get-tuple-element.364) | copy-start | bytes 25165828 | tf_op jit(solution)/shard_map/while
  948.6 33.0 %copy-start.2 = (f32[4,4,32,4096]{3,2,1,0:T(8,128)S(1)}, f32[4,4,32,4096]{3,2,1,0:T(8,128)}, u32[]{:S(2)}) copy-start(f32[4,4,32,4096]{3,2,1,0:T(8,128)} %get-tuple-element.364) | copy-start | bytes 25165828 | tf_op jit(solution)/shard_map/while
  998.0 33.0 %copy-start.2 = (f32[4,4,32,4096]{3,2,1,0:T(8,128)S(1)}, f32[4,4,32,4096]{3,2,1,0:T(8,128)}, u32[]{:S(2)}) copy-start(f32[4,4,32,4096]{3,2,1,0:T(8,128)} %get-tuple-element.364) | copy-start | bytes 25165828 | tf_op jit(solution)/shard_map/while
  1047.3 33.0 %copy-start.2 = (f32[4,4,32,4096]{3,2,1,0:T(8,128)S(1)}, f32[4,4,32,4096]{3,2,1,0:T(8,128)}, u32[]{:S(2)}) copy-start(f32[4,4,32,4096]{3,2,1,0:T(8,128)} %get-tuple-element.364) | copy-start | bytes 25165828 | tf_op jit(solution)/shard_map/while
  1097.1 192.1 %all-to-all-start.1 = ((f32[32,4,32,512]{3,2,1,0:T(8,128)}), f32[32,4,32,512]{3,2,1,0:T(8,128)}, u32[]{:S(2)}, u32[]{:S(2)}) async-start(f32[32,4,32,512]{3,2,1,0:T(8,128)} %bitcast.8), calls=%async_computation.1 | async-start | bytes 16777216 | tf_op jit(solution)/shard_map/all_to_all | solution.py:165
  1102.9 292.4 %all-reduce.7.cloned.1.call-start = ((), (), s32[]{:S(2)}) async-start(), calls=%async_computation.2 | async-start | bytes 4194304 | tf_op jit(solution)/shard_map/psum | solution.py:16
  1114.3 36.4 %collective-permute-start = (f32[16,1,512]{2,1,0:T(1,128)S(1)}, f32[16,1,512]{2,1,0:T(1,128)S(1)}, u32[]{:S(2)}, u32[]{:S(2)}) collective-permute-start(f32[16,1,512]{2,1,0:T(1,128)S(1)} %get-tuple-element.287), channel_id=1, source_target_pairs={{0,8},{8,16},{16,24},{24,0},{1,9},{9,17},{17,25},{25,1},{2,10},{10... | collective-permute-start | bytes 98312 | tf_op jit(solution)/shard_map/ppermute | solution.py:26
  1114.6 36.2 %collective-permute-start.2 = (f32[16,1,512]{2,1,0:T(1,128)S(1)}, f32[16,1,512]{2,1,0:T(1,128)S(1)}, u32[]{:S(2)}, u32[]{:S(2)}) collective-permute-start(f32[16,1,512]{2,1,0:T(1,128)S(1)} %get-tuple-element.288), channel_id=1, source_target_pairs={{8,0},{16,8},{24,16},{0,24},{9,1},{17,9},{25,17},{1,25},{10,2},{18... | collective-permute-start | bytes 98312 | tf_op jit(solution)/shard_map/ppermute | solution.py:28
  1117.2 226.0 %collective-permute-start.1 = (f32[16,1,512]{2,1,0:T(1,128)S(1)}, f32[16,1,512]{2,1,0:T(1,128)S(1)}, u32[]{:S(2)}, u32[]{:S(2)}) collective-permute-start(f32[16,1,512]{2,1,0:T(1,128)S(1)} %get-tuple-element.289), channel_id=1, source_target_pairs={{0,8},{8,16},{16,24},{24,0},{1,9},{9,17},{17,25},{25,1},{2,10},{10... | collective-permute-start | bytes 98312 | tf_op jit(solution)/shard_map/ppermute | solution.py:26
  1117.3 225.9 %collective-permute-start.3 = (f32[16,1,512]{2,1,0:T(1,128)S(1)}, f32[16,1,512]{2,1,0:T(1,128)S(1)}, u32[]{:S(2)}, u32[]{:S(2)}) collective-permute-start(f32[16,1,512]{2,1,0:T(1,128)S(1)} %get-tuple-element.290), channel_id=1, source_target_pairs={{8,0},{16,8},{24,16},{0,24},{9,1},{17,9},{25,17},{1,25},{10,2},{18... | collective-permute-start | bytes 98312 | tf_op jit(solution)/shard_map/ppermute | solution.py:28
  1157.6 214.0 %collective-permute-start.4 = (f32[16,258,1]{1,0,2:T(8,128)S(1)}, f32[16,258,1]{1,0,2:T(8,128)S(1)}, u32[]{:S(2)}, u32[]{:S(2)}) collective-permute-start(f32[16,258,1]{1,0,2:T(8,128)S(1)} %copy.33), channel_id=1, source_target_pairs={{0,1},{1,2},{2,3},{3,4},{4,5},{5,6},{6,7},{7,0},{8,9},{9,10},{10,1... | collective-permute-start | bytes 49544 | tf_op jit(solution)/shard_map/ppermute | solution.py:26
  1158.5 213.8 %collective-permute-start.6 = (f32[16,258,1]{1,0,2:T(8,128)S(1)}, f32[16,258,1]{1,0,2:T(8,128)S(1)}, u32[]{:S(2)}, u32[]{:S(2)}) collective-permute-start(f32[16,258,1]{1,0,2:T(8,128)S(1)} %copy.37), channel_id=1, source_target_pairs={{1,0},{2,1},{3,2},{4,3},{5,4},{6,5},{7,6},{0,7},{9,8},{10,9},{11,1... | collective-permute-start | bytes 49544 | tf_op jit(solution)/shard_map/ppermute | solution.py:28
  1350.1 24.4 %collective-permute-start.5 = (f32[16,258,1]{1,0,2:T(8,128)S(1)}, f32[16,258,1]{1,0,2:T(8,128)S(1)}, u32[]{:S(2)}, u32[]{:S(2)}) collective-permute-start(f32[16,258,1]{1,0,2:T(8,128)S(1)} %copy.35), channel_id=1, source_target_pairs={{0,1},{1,2},{2,3},{3,4},{4,5},{5,6},{6,7},{7,0},{8,9},{9,10},{10,1... | collective-permute-start | bytes 49544 | tf_op jit(solution)/shard_map/ppermute | solution.py:26
  1352.9 23.6 %collective-permute-start.7 = (f32[16,258,1]{1,0,2:T(8,128)S(1)}, f32[16,258,1]{1,0,2:T(8,128)S(1)}, u32[]{:S(2)}, u32[]{:S(2)}) collective-permute-start(f32[16,258,1]{1,0,2:T(8,128)S(1)} %copy.39), channel_id=1, source_target_pairs={{1,0},{2,1},{3,2},{4,3},{5,4},{6,5},{7,6},{0,7},{9,8},{10,9},{11,1... | collective-permute-start | bytes 49544 | tf_op jit(solution)/shard_map/ppermute | solution.py:28
  1371.6 23.7 %copy-start.3 = (f32[256,512]{1,0:T(8,128)S(1)}, f32[256,512]{1,0:T(8,128)}, u32[]{:S(2)}) copy-start(f32[256,512]{1,0:T(8,128)} %param.11) | copy-start | bytes 1572868
  1445.0 3.4 collective-permute-start.8
  1445.1 3.3 collective-permute-start.9
  1456.0 23.0 %collective-permute-start.10 = (f32[16,258,1]{1,0,2:T(8,128)S(1)}, f32[16,258,1]{1,0,2:T(8,128)S(1)}, u32[]{:S(2)}, u32[]{:S(2)}) collective-permute-start(f32[16,258,1]{1,0,2:T(8,128)S(1)} %copy.41), channel_id=1, source_target_pairs={{0,1},{1,2},{2,3},{3,4},{4,5},{5,6},{6,7},{7,0},{8,9},{9,10},{10,1... | collective-permute-start | bytes 49544 | tf_op jit(solution)/shard_map/ppermute | solution.py:26
  1460.2 20.9 %collective-permute-start.11 = (f32[16,258,1]{1,0,2:T(8,128)S(1)}, f32[16,258,1]{1,0,2:T(8,128)S(1)}, u32[]{:S(2)}, u32[]{:S(2)}) collective-permute-start(f32[16,258,1]{1,0,2:T(8,128)S(1)} %copy.43), channel_id=1, source_target_pairs={{1,0},{2,1},{3,2},{4,3},{5,4},{6,5},{7,6},{0,7},{9,8},{10,9},{11,1... | collective-permute-start | bytes 49544 | tf_op jit(solution)/shard_map/ppermute | solution.py:28
  (3 other events, 12.5 us)
Sparse Core Ops, SparseCore 0:
  1343.3 51.9 all-reduce.6
where the time goes:
time: 1550 us; the launch traced here: 1540 us
  other arithmetic  698 us (45%)
  matrix products  365 us (24%)
  waiting for transfers between devices  362 us (23%)
  local copies, waits for them, and re-layouts  64.2 us (4%)
  starting transfers between devices  33.1 us (2%)
    dot_general x8, other arithmetic, forward_block(): jnp.einsum(form_in, blocked, table_part, precision=HIGHEST, preferred_ele...  265 us
    dot_general x8, other arithmetic, backward_block(): jnp.einsum('gzkx,xqm->gqzkm', solved_groups, table_part, precision=HIGHES...  264 us
    all_to_all x1, waiting for transfers between devices, per_device(): lax.all_to_all(spectral.reshape(1, depth_loc, span_len, stream_loc), ('gr...  186 us
    dot_general x8, matrix products, forward_block(): jnp.einsum(form_in, blocked, table_part, precision=HIGHEST, preferred_ele...  132 us
    dot_general x8, matrix products, backward_block(): jnp.einsum('gzkx,xqm->gqzkm', solved_groups, table_part, precision=HIGHES...  131 us
    all_to_all x1, waiting for transfers between devices, per_device(): lax.all_to_all(physical.reshape(groups * pencils, depth_loc, span_loc, st...  126 us
    add x2, other arithmetic, conduct(): return centre_temp + STEP_RATE * (net_flux + surface)  94.7 us
    dot_general x1, matrix products, per_device(): jnp.einsum('zyx,yw->zwx', pressure_source, span_table, precision=HIGHEST,...  56.9 us
  transfers between devices with their start and end apart: 15, of which 5 were waited for; matrix products, arithmetic and copies ran while one was open for 8% of the time, Pallas kernels for 0%

commit v1 on v0

v1 whole, which is shorter than its diff:
```python
import functools
import math

import jax
import jax.numpy as jnp
import numpy as np
from jax import lax
from jax.experimental import pallas as pl
from jax.experimental.pallas import tpu as pltpu
from jax.sharding import PartitionSpec as P

HIGH = lax.Precision.HIGH
HEAT_TRANSFER = 1.0
PRESSURE_WORK = 0.5
STEP_RATE = 0.12
LANES = 128
SEGMENTS = 8
VMEM_BYTES = 56 * 2**20


def params():
    return pltpu.CompilerParams(vmem_limit_bytes=VMEM_BYTES)


def with_halo(cells, sides, width):
    for axis, dim in sides:
        count = lax.axis_size(axis)
        head = lax.slice_in_dim(cells, 0, width, axis=dim)
        tail = lax.slice_in_dim(cells, cells.shape[dim] - width, cells.shape[dim], axis=dim)
        cells = jnp.concatenate(
            [
                lax.ppermute(tail, axis, [(i, (i + 1) % count) for i in range(count)]),
                cells,
                lax.ppermute(head, axis, [((i + 1) % count, i) for i in range(count)]),
            ],
            axis=dim,
        )
    return cells


def cas(product, length):
    angle = (product % length) * (2.0 * math.pi / length)
    return np.cos(angle) + np.sin(angle)


def depth_modes(depth_len):
    matrix = np.diag(np.full(depth_len, -2.0))
    matrix += np.diag(np.ones(depth_len - 1), 1) + np.diag(np.ones(depth_len - 1), -1)
    matrix[0, 0] = -1.0
    values, vectors = np.linalg.eigh(matrix)
    return -values, vectors.T


def wave_order(span_len, groups):
    order = np.concatenate([np.arange(0, span_len, 2), np.arange(1, span_len, 2)])
    return order.reshape(groups, span_len // groups)


def split(value):
    high = value.astype(jnp.bfloat16)
    low = (value - high.astype(jnp.float32)).astype(jnp.bfloat16)
    return high, low


def dot_split(left, right, dims):
    dot = functools.partial(
        lax.dot_general, dimension_numbers=(dims, ((), ())), preferred_element_type=jnp.float32
    )
    return dot(left[0], right[0]) + dot(left[0], right[1]) + dot(left[1], right[0])


def span_forward_kernel(source_ref, table_ref, out_ref):
    half = table_ref.shape[2]
    width = out_ref.shape[3]
    head = source_ref[0, :half]
    tail = source_ref[0, half:]
    for parity in range(2):
        folded = split(head - tail if parity else head + tail)
        table = (table_ref[parity, 0], table_ref[parity, 1])
        result = dot_split(folded, table, ((0,), (0,)))
        per = half // width
        for part in range(per):
            out_ref[parity * per + part, 0] = result[:, part * width : (part + 1) * width]


def span_inverse_kernel(waves_ref, table_ref, out_ref):
    half = table_ref.shape[2]
    per = waves_ref.shape[0] // 2
    halves = []
    for parity in range(2):
        table = (table_ref[parity, 0], table_ref[parity, 1])
        waves = jnp.concatenate([waves_ref[parity * per + part, 0] for part in range(per)], axis=1)
        halves.append(dot_split(table, split(waves), ((1,), (1,))))
    out_ref[0, :half] = halves[0] + halves[1]
    out_ref[0, half:] = halves[0] - halves[1]


def mix(weights, planes):
    result = []
    for row in weights:
        total = float(row[0]) * planes[0]
        for weight, plane in zip(row[1:], planes[1:]):
            total = total + float(weight) * plane
        result.append(total)
    return result


def ends_kernel(vectors, source_ref, root_ref, modes_ref, head_ref, tail_ref):
    depth_len, steps = modes_ref.shape[0], modes_ref.shape[1]

    def ahead(step, carry):
        planes = [
            source_ref[plane, pl.ds(step, SEGMENTS, stride=steps), :] for plane in range(depth_len)
        ]
        made = []
        for mode, value in enumerate(mix(vectors, planes)):
            modes_ref[mode, step] = value
            made.append(value + root_ref[mode][None] * carry[mode])
        return tuple(made)

    def back(step, carry):
        return tuple(
            modes_ref[mode, steps - 1 - step] + root_ref[mode][None] * carry[mode]
            for mode in range(depth_len)
        )

    zero = tuple(jnp.zeros((SEGMENTS, LANES), jnp.float32) for _ in range(depth_len))
    ended = lax.fori_loop(0, steps, ahead, zero)
    for mode in range(depth_len):
        tail_ref[mode] = ended[mode]
    ended = lax.fori_loop(0, steps, back, zero)
    for mode in range(depth_len):
        head_ref[mode] = ended[mode]


def solve_kernel(vectors, modes_ref, root_ref, gain_ref, left_ref, right_ref, out_ref, ahead_ref):
    depth_len, steps = modes_ref.shape[0], modes_ref.shape[1]

    def ahead(step, carry):
        made = []
        for mode in range(depth_len):
            value = modes_ref[mode, step] + root_ref[mode][None] * carry[mode]
            ahead_ref[mode, step] = value
            made.append(value)
        return tuple(made)

    def back(count, carry):
        step = steps - 1 - count
        made, solved = [], []
        for mode in range(depth_len):
            coming = root_ref[mode][None] * carry[mode]
            solved.append(gain_ref[mode][None] * (ahead_ref[mode, step] + coming))
            made.append(modes_ref[mode, step] + coming)
        for plane, value in enumerate(mix(vectors.T, solved)):
            out_ref[plane, pl.ds(step, SEGMENTS, stride=steps), :] = value
        return tuple(made)

    lax.fori_loop(0, steps, ahead, tuple(left_ref[mode] for mode in range(depth_len)))
    lax.fori_loop(0, steps, back, tuple(right_ref[mode] for mode in range(depth_len)))


def conduct(padded_temp, padded_cond):
    centre_temp = padded_temp[:, 1:-1, 1:-1]
    centre_cond = padded_cond[:, 1:-1, 1:-1]
    net_flux = jnp.zeros_like(centre_temp)
    neighbours = (
        (padded_temp[:, :-2, 1:-1], padded_cond[:, :-2, 1:-1]),
        (padded_temp[:, 2:, 1:-1], padded_cond[:, 2:, 1:-1]),
        (padded_temp[:, 1:-1, :-2], padded_cond[:, 1:-1, :-2]),
        (padded_temp[:, 1:-1, 2:], padded_cond[:, 1:-1, 2:]),
    )
    for shift_temp, shift_cond in neighbours:
        net_flux = net_flux + 0.5 * (centre_cond + shift_cond) * (shift_temp - centre_temp)
    if centre_temp.shape[0] > 1:
        vertical = 0.5 * (centre_cond[1:] + centre_cond[:-1]) * (centre_temp[1:] - centre_temp[:-1])
        net_flux = (
            net_flux
            + jnp.pad(vertical, ((0, 1), (0, 0), (0, 0)))
            - jnp.pad(vertical, ((1, 0), (0, 0), (0, 0)))
        )
    return centre_temp + STEP_RATE * net_flux


def per_device(pressure_source, solid_temp, gas_wall_temp, phase_map, phase_conductivity):
    groups = lax.axis_size("grp")
    pencils = lax.axis_size("pen")
    group_idx = lax.axis_index("grp")
    pencil_idx = lax.axis_index("pen")
    depth_loc, span_len, stream_loc = pressure_source.shape
    stream_len = stream_loc * pencils
    depth_len = depth_loc * groups
    half = span_len // 2
    waves_loc = span_len // groups
    steps = stream_loc // SEGMENTS
    f32 = jnp.float32

    order = wave_order(span_len, groups)
    row = np.arange(half)
    table = np.stack([cas(row[:, None] * (2 * row + parity)[None, :], span_len) for parity in (0, 1)])
    table_high = table.astype(jnp.bfloat16)
    table_low = (table - table_high.astype(np.float64)).astype(jnp.bfloat16)
    table_parts = jnp.asarray(np.stack([table_high, table_low], axis=1))
    lambdas, vectors = depth_modes(depth_len)
    eigen_span = 2.0 * np.cos(2.0 * math.pi * order / span_len) - 2.0
    shift = lambdas[None, :, None] - eigen_span[:, None, :]
    root = 2.0 / (shift + 2.0 + np.sqrt(shift * (shift + 4.0)))
    gain = -1.0 / (1.0 / root - root) / span_len
    around = np.arange(pencils)[:, None, None, None]
    reach = np.power(root, stream_loc * around) / (1.0 - np.power(root, stream_len))

    def mine(constant, axis):
        chosen = lax.dynamic_index_in_dim(jnp.asarray(constant, f32), group_idx, axis, keepdims=False)
        return chosen

    root_loc = mine(root, 0)
    gain_loc = mine(gain, 0)
    hop_loc = mine(np.power(root, steps), 0)
    reach_loc = mine(reach, 1)
    falling = jnp.roll(jnp.flip(reach_loc, 0), 1, 0)
    reach_left = lax.dynamic_slice_in_dim(
        jnp.concatenate([falling, falling]), (pencils + 1 - pencil_idx) % pencils, pencils, 0
    )
    reach_right = lax.dynamic_slice_in_dim(
        jnp.concatenate([reach_loc, reach_loc]), (2 * pencils - 1 - pencil_idx) % pencils, pencils, 0
    )

    spectral = pl.pallas_call(
        span_forward_kernel,
        grid=(depth_loc,),
        in_specs=[
            pl.BlockSpec((1, span_len, stream_loc), lambda z: (z, 0, 0)),
            pl.BlockSpec((2, 2, half, half), lambda z: (0, 0, 0, 0)),
        ],
        out_specs=pl.BlockSpec((groups, 1, stream_loc, waves_loc), lambda z: (0, z, 0, 0)),
        out_shape=jax.ShapeDtypeStruct((groups, depth_loc, stream_loc, waves_loc), f32),
        compiler_params=params(),
        cost_estimate=pl.CostEstimate(
            flops=6 * depth_loc * stream_loc * span_len * half,
            bytes_accessed=8 * depth_loc * stream_loc * span_len,
            transcendentals=0,
        ),
        name="span_forward",
    )(pressure_source, table_parts)
    moved = lax.all_to_all(spectral, "grp", split_axis=0, concat_axis=0, tiled=True)
    moved = moved.reshape(depth_len, stream_loc, waves_loc)

    data_spec = pl.BlockSpec((depth_len, stream_loc, LANES), lambda w: (0, 0, w))
    mode_spec = pl.BlockSpec((depth_len, steps, SEGMENTS, LANES), lambda w: (0, 0, 0, w))
    wave_spec = pl.BlockSpec((depth_len, 1, LANES), lambda w: (0, 0, w))
    ends_spec = pl.BlockSpec((depth_len, SEGMENTS, LANES), lambda w: (0, 0, w))
    ends_shape = jax.ShapeDtypeStruct((depth_len, SEGMENTS, waves_loc), f32)
    cost = pl.CostEstimate(
        flops=2 * depth_len**2 * stream_loc * waves_loc,
        bytes_accessed=8 * depth_len * stream_loc * waves_loc,
        transcendentals=0,
    )

    def rowed(value):
        return value[:, None, :]

    modes, heads, tails = pl.pallas_call(
        lambda s, r, m, h, t: ends_kernel(vectors, s, FirstRow(r), m, h, t),
        grid=(waves_loc // LANES,),
        in_specs=[data_spec, wave_spec],
        out_specs=[mode_spec, ends_spec, ends_spec],
        out_shape=[
            jax.ShapeDtypeStruct((depth_len, steps, SEGMENTS, waves_loc), f32),
            ends_shape,
            ends_shape,
        ],
        compiler_params=params(),
        cost_estimate=cost,
        name="stream_ends",
    )(moved, rowed(root_loc))
    tail_all = tails[:, 0]
    head_all = heads[:, SEGMENTS - 1]
    for part in range(1, SEGMENTS):
        tail_all = tails[:, part] + hop_loc * tail_all
        head_all = heads[:, SEGMENTS - 1 - part] + hop_loc * head_all
    gathered = lax.all_gather(jnp.stack([tail_all, head_all]), "pen")
    left = [jnp.sum(reach_left * gathered[:, 0], axis=0)]
    right = [jnp.sum(reach_right * gathered[:, 1], axis=0)]
    for part in range(SEGMENTS - 1):
        left.append(tails[:, part] + hop_loc * left[-1])
        right.append(heads[:, SEGMENTS - 1 - part] + hop_loc * right[-1])
    solved = pl.pallas_call(
        lambda m, r, g, a, b, o, c: solve_kernel(vectors, m, FirstRow(r), FirstRow(g), a, b, o, c),
        grid=(waves_loc // LANES,),
        in_specs=[mode_spec, wave_spec, wave_spec, ends_spec, ends_spec],
        out_specs=data_spec,
        out_shape=jax.ShapeDtypeStruct((depth_len, stream_loc, waves_loc), f32),
        scratch_shapes=[pltpu.VMEM((depth_len, steps, SEGMENTS, LANES), f32)],
        compiler_params=params(),
        cost_estimate=cost,
        name="stream_solve",
    )(modes, rowed(root_loc), rowed(gain_loc), jnp.stack(left, 1), jnp.stack(right[::-1], 1))

    returned = lax.all_to_all(
        solved.reshape(groups, depth_loc, stream_loc, waves_loc),
        "grp",
        split_axis=0,
        concat_axis=0,
        tiled=True,
    )
    pressure = pl.pallas_call(
        span_inverse_kernel,
        grid=(depth_loc,),
        in_specs=[
            pl.BlockSpec((groups, 1, stream_loc, waves_loc), lambda z: (0, z, 0, 0)),
            pl.BlockSpec((2, 2, half, half), lambda z: (0, 0, 0, 0)),
        ],
        out_specs=pl.BlockSpec((1, span_len, stream_loc), lambda z: (z, 0, 0)),
        out_shape=jax.ShapeDtypeStruct((depth_loc, span_len, stream_loc), f32),
        compiler_params=params(),
        cost_estimate=pl.CostEstimate(
            flops=6 * depth_loc * stream_loc * span_len * half,
            bytes_accessed=8 * depth_loc * stream_loc * span_len,
            transcendentals=0,
        ),
        name="span_inverse",
    )(returned, table_parts)

    tile_rows = span_len // groups
    sides = (("grp", 1), ("pen", 2))
    cell_cond = jnp.where(phase_map == 1, phase_conductivity[1], phase_conductivity[0])
    padded_temp, padded_cond = with_halo(solid_temp, sides, 1), with_halo(cell_cond, sides, 1)
    first_temp = conduct(padded_temp, padded_cond)
    unheated = conduct(with_halo(first_temp, sides, 1), padded_cond)
    dry_flux = with_halo((gas_wall_temp - solid_temp[0])[None], sides, 1)

    span_rows = np.arange(-1, span_len + 1) % span_len
    wall_table = cas(span_rows[:, None] * order.reshape(1, -1), span_len)
    wall_rows = lax.dynamic_slice_in_dim(
        jnp.asarray(wall_table, f32), group_idx * tile_rows, tile_rows + 2, 0
    )
    wall_waves = lax.all_gather(solved[0], "grp")
    wall = jnp.einsum(
        "ygk,gxk->yx",
        wall_rows.reshape(tile_rows + 2, groups, waves_loc),
        wall_waves,
        precision=HIGH,
        preferred_element_type=f32,
    )
    wall = with_halo(wall[None], (("pen", 2),), 1)
    flux = HEAT_TRANSFER * (dry_flux + PRESSURE_WORK * wall)
    centre_flux = flux[0, 1:-1, 1:-1]
    between = 0.5 * (padded_cond[0] + padded_cond[1])[1:-1, 1:-1] * centre_flux
    lateral = conduct(flux, padded_cond[:1])[0]
    top = STEP_RATE * (centre_flux + lateral - STEP_RATE * between)
    second = STEP_RATE * STEP_RATE * between
    final_temp = unheated.at[0].add(top).at[1].add(second)
    return (pressure, final_temp)


class FirstRow:
    def __init__(self, ref):
        self.ref = ref

    def __getitem__(self, mode):
        return self.ref[mode, 0]


def solution(mesh):
    in_specs = (
        P("grp", None, "pen"),
        P(None, "grp", "pen"),
        P("grp", "pen"),
        P(None, "grp", "pen"),
        P(),
    )
    out_specs = (P("grp", None, "pen"), P(None, "grp", "pen"))
    return jax.shard_map(
        per_device, mesh=mesh, in_specs=in_specs, out_specs=out_specs, check_vma=False
    )
```

time: 1550 us -> 434 us (0.28)
  other arithmetic: 698 us -> 178 us
  matrix products: 365 us -> 3.01 us
  waiting for transfers between devices: 362 us -> 54.9 us
  Pallas kernels: 0 us -> 68.9 us
  blocking collectives: 0 us -> 30.7 us
  local copies, waits for them, and re-layouts: 64.2 us -> 40 us
    dot_general x16 -> x0, other arithmetic: 528 us -> none  [the longest x8 265 us: forward_block(): jnp.einsum(form_in, blocked, table_part, precision=HIGHEST, preferred_ele...]
    dot_general x18 -> x1, matrix products: 365 us -> 3.01 us  [per_device(): jnp.einsum('ygk,gxk->yx', wall_rows.reshape(tile_rows + 2, groups, waves_...]
    all_to_all x2, waiting for transfers between devices: 312 us -> 0.01 us  [the longest x1 0.01 us: per_device(): lax.all_to_all(spectral, 'grp', split_axis=0, concat_axis=0, tiled=True)]
    pallas_call x0 -> x4, Pallas kernels: none -> 68.9 us  [the longest x1 24 us: per_device(): pl.pallas_call(lambda s, r, m, h, t: ends_kernel(vectors, s, FirstRow(r),...]
    all_gather x0 -> x1, blocking collectives: none -> 30.7 us  [per_device(): gathered = lax.all_gather(jnp.stack([tail_all, head_all]), 'pen')]
    ppermute x6 -> x9, waiting for transfers between devices: 33.3 us -> 54.9 us  [with_halo(): lax.ppermute(tail, axis, [(i, (i + 1) % count) for i in range(count)])]
    psum x1 -> x0, waiting for transfers between devices: 16.7 us -> none  [broadcast(): return lax.psum(kept, axis)]
    concatenate x0 -> x1, other arithmetic: none -> 16.3 us  [with_halo(): jnp.concatenate([lax.ppermute(tail, axis, [(i, (i + 1) % count) for i in...]
  transfers between devices with their start and end apart: 15 -> 21, of which waited for: 5 -> 1; matrix products, arithmetic and copies ran while one was open for 8% -> 50% of each run, Pallas kernels for 0% -> 10%
where the time goes in v1:
time: 434 us; the launch traced here: 433 us
  other arithmetic  178 us (41%)
  Pallas kernels  68.9 us (16%)
  waiting for transfers between devices  54.9 us (13%)
  starting transfers between devices  43 us (10%)
  local copies, waits for them, and re-layouts  40 us (9%)
  blocking collectives  30.7 us (7%)
  between operations  14.3 us (3%)
    add x2, other arithmetic, conduct(): return centre_temp + STEP_RATE * net_flux  93.5 us
    ppermute x9, waiting for transfers between devices, with_halo(): lax.ppermute(tail, axis, [(i, (i + 1) % count) for i in range(count)])  54.9 us
    mul x2, other arithmetic, conduct(): 0.5 * (centre_cond[1:] + centre_cond[:-1])  31.2 us
    all_gather x1, blocking collectives, per_device(): gathered = lax.all_gather(jnp.stack([tail_all, head_all]), 'pen')  30.7 us
    ppermute x9, starting transfers between devices, with_halo(): lax.ppermute(head, axis, [((i + 1) % count, i) for i in range(count)])  27 us
    pallas_call x1, Pallas kernels, per_device(): pl.pallas_call(lambda s, r, m, h, t: ends_kernel(vectors, s, FirstRow(r),...  24 us
    pallas_call x1, Pallas kernels, per_device(): pl.pallas_call(lambda m, r, g, a, b, o, c: solve_kernel(vectors, m, First...  21.3 us
    concatenate x1, other arithmetic, with_halo(): jnp.concatenate([lax.ppermute(tail, axis, [(i, (i + 1) % count) for i in...  16.3 us
  transfers between devices with their start and end apart: 21, of which 1 were waited for; matrix products, arithmetic and copies ran while one was open for 50% of the time, Pallas kernels for 10%

profile of v1, /device:TPU:0, one launch (start us, length us, event | category | flops | bytes accessed | tf_op | source)
XLA Modules:
  0.0 432.6 jit_solution(997189962940235536)
XLA Ops:
  7.2 12.0 %span_forward.1 = f32[4,4,512,256]{3,2,1,0:T(8,128)} custom-call(f32[4,1024,512]{2,1,0:T(8,128)} %source_ref.1, bf16[2,2,512,512]{3,2,1,0:T(8,128)(2,1)} %constant.131.clone.table_ref), custom_call_target="tpu_custom_call" | custom-call | flops 6442450944 | bytes 16777216 | tf_op jit(solution)/shard_map/span_forward/pallas_call | solution.py:227
  19.1 5.7 %all-to-all-start = ((f32[4,4,512,256]{3,2,1,0:T(8,128)}), f32[4,4,512,256]{3,2,1,0:T(8,128)}, u32[]{:S(2)}, u32[]{:S(2)}) async-start(f32[4,4,512,256]{3,2,1,0:T(8,128)} %span_forward.1), calls=%async_computation | async-start | bytes 16777216 | tf_op jit(solution)/shard_map/all_to_all | solution.py:244
  25.6 7.7 %broadcast_select_fusion = (f32[16,256,512]{2,1,0:T(8,128)S(1)}, pred[16,256,512]{2,1,0:T(8,128)(4,1)}) fusion(f32[]{:T(128)} %bitcast.28, f32[]{:T(128)} %bitcast.27, s32[16,256,512]{2,1,0:T(8,128)} %param.18), kind=kLoop, calls=%fused_computation.67 | loop fusion | flops 4194304 | bytes 18874376 | tf_op jit(solution)/shard_map/jit(_where)/select_n | solution.py:325
  33.2 3.4 copy-done
  45.3 15.5 %subtract_multiply_fusion = f32[15,256,512]{2,1,0:T(8,128)} fusion(f32[16,256,512]{2,1,0:T(8,128)} %param.16, f32[16,256,512]{2,1,0:T(8,128)} %copy-done), kind=kLoop, calls=%fused_computation.66 | loop fusion | flops 7864320 | bytes 39321600 | tf_op jit(solution)/shard_map/mul | solution.py:175
  63.7 54.8 %collective-permute-done = f32[16,1,512]{2,1,0:T(1,128)S(1)} collective-permute-done((f32[16,1,512]{2,1,0:T(1,128)S(1)}, f32[16,1,512]{2,1,0:T(1,128)S(1)}, u32[]{:S(2)}, u32[]{:S(2)}) %collective-permute-start) | collective-permute-done | bytes 32800 | tf_op jit(solution)/shard_map/ppermute | solution.py:32
  118.6 4.3 pad_maximum_fusion.25
  122.9 2.5 copy.15
  125.4 2.6 collective-permute-start.4
  128.9 3.1 collective-permute-start.6
  132.0 4.3 pad_maximum_fusion.24
  136.3 2.5 copy.17
  139.8 4.7 %collective-permute-start.7 = (f32[16,258,1]{1,0,2:T(8,128)S(1)}, f32[16,258,1]{1,0,2:T(8,128)S(1)}, u32[]{:S(2)}, u32[]{:S(2)}) collective-permute-start(f32[16,258,1]{1,0,2:T(8,128)S(1)} %copy.21), channel_id=1, source_target_pairs={{1,0},{2,1},{3,2},{4,3},{5,4},{6,5},{7,6},{0,7},{9,8},{10,9},{11,1... | collective-permute-start | bytes 49544 | tf_op jit(solution)/shard_map/ppermute | solution.py:34
  145.3 4.7 %collective-permute-start.15 = (f32[1,258,1]{2,1,0:T(8,128)}, f32[1,258,1]{2,1,0:T(8,128)}, u32[]{:S(2)}, u32[]{:S(2)}) collective-permute-start(f32[1,258,1]{2,1,0:T(8,128)} %get-tuple-element.67), channel_id=1, source_target_pairs={{1,0},{2,1},{3,2},{4,3},{5,4},{6,5},{7,6},{0,7},{9,8},{10,9},{11,1... | collective-permute-start | bytes 3104 | tf_op jit(solution)/shard_map/ppermute | solution.py:34
  157.0 16.3 %maximum_maximum_fusion = (f32[16,258,513]{2,1,0:T(8,128)}, f32[16,258,513]{2,1,0:T(8,128)}) fusion(f32[16,1,512]{2,1,0:T(1,128)S(1)} %collective-permute-done.2, f32[16,256,512]{2,1,0:T(8,128)} %copy-done, f32[16,1,512]{2,1,0:T(1,128)S(1)} %collective-permute-done, f32[16,258,1]{2,1,0:T(8,128)S(1)} %copy.16, f32[16,258,1]{2,1,0:T(8,128)} %copy.20), kind=kLoop, calls=%fused_computation | loop fusion | flops 12705984 | bytes 25428480 | tf_op jit(solution)/shard_map/concatenate | solution.py:30
  173.3 24.0 %stream_ends.1 = (f32[16,64,8,256]{3,2,1,0:T(8,128)}, f32[16,8,256]{2,1,0:T(8,128)}, f32[16,8,256]{2,1,0:T(8,128)}) custom-call(f32[16,512,256]{2,1,0:T(8,128)} %bitcast.s, f32[16,1,256]{2,1,0:T(1,128)} %dynamic-slice_bitcast_fusion.5.r), custom_call_target="tpu_custom_call" | custom-call | flops 67108864 | bytes 16777216 | tf_op jit(solution)/shard_map/stream_ends/pallas_call | solution.py:261
  197.3 3.2 fusion.105
  200.6 30.7 %all-gather = f32[16,16,256]{2,1,0:T(8,128)S(1)} all-gather(f32[2,16,256]{2,1,0:T(8,128)S(1)} %copy.14), channel_id=2, replica_groups=mesh['grp'=4,'pen'=8] {'pen'}, dimensions={0}, use_global_device_ids=true | all-gather | bytes 294912 | tf_op jit(solution)/shard_map/all_gather | solution.py:280
  235.5 21.3 %stream_solve.1 = f32[16,512,256]{2,1,0:T(8,128)} custom-call(f32[16,64,8,256]{3,2,1,0:T(8,128)} %get-tuple-element.29.m, f32[16,1,256]{2,1,0:T(1,128)} %dynamic-slice_bitcast_fusion.5.r, f32[16,1,256]{2,1,0:T(1,128)} %get-tuple-element.81.g, f32[16,8,256]{2,1,0:T(8,128)} %stack.10.a, f32[16,8,256]{2,1,0:T(8,128)} %stack.11.b), custom_call_target="tpu_custom_call" | custom-call | flops 67108864 | bytes 16777216 | tf_op jit(solution)/shard_map/stream_solve/pallas_call | solution.py:286
  258.7 46.6 %fusion.27 = f32[16,256,512]{2,1,0:T(8,128)} fusion(f32[16,256,512]{2,1,0:T(8,128)} %param.16, f32[16,258,1]{2,1,0:T(8,128)} %copy.22, f32[16,1,512]{2,1,0:T(1,128)S(1)} %collective-permute-done.3, f32[16,1,512]{2,1,0:T(1,128)S(1)} %collective-permute-done.1, f32[16,258,1]{2,1,0:T(8,128)} %copy.18, f32[15,256,512]{2,1,0:T(8,128)} %subtract_multiply_fusion, ...), kind=kLoop, calls=%fused_computation.46 | loop fusion | flops 71303168 | bytes 52068616 | tf_op jit(solution)/shard_map/add | solution.py:181
  308.2 5.8 %all-to-all-start.1 = ((f32[4,4,512,256]{3,2,1,0:T(8,128)}), f32[4,4,512,256]{3,2,1,0:T(8,128)}, u32[]{:S(2)}, u32[]{:S(2)}) async-start(f32[4,4,512,256]{3,2,1,0:T(8,128)} %bitcast.226), calls=%async_computation.1 | async-start | bytes 16777216 | tf_op jit(solution)/shard_map/all_to_all | solution.py:298
  314.1 15.7 %fusion.36 = f32[15,256,512]{2,1,0:T(8,128)} fusion(f32[16,256,512]{2,1,0:T(8,128)} %fusion.27, f32[16,256,512]{2,1,0:T(8,128)} %copy-done), kind=kLoop, calls=%fused_computation.63 | loop fusion | flops 7864320 | bytes 39321600 | tf_op jit(solution)/shard_map/mul | solution.py:175
  329.8 2.9 pad_maximum_fusion.19
  332.7 2.5 copy.23
  335.2 3.1 copy.25
  338.3 4.7 %collective-permute-start.11 = (f32[16,258,1]{1,0,2:T(8,128)}, f32[16,258,1]{1,0,2:T(8,128)}, u32[]{:S(2)}, u32[]{:S(2)}) collective-permute-start(f32[16,258,1]{1,0,2:T(8,128)} %copy.25), channel_id=1, source_target_pairs={{1,0},{2,1},{3,2},{4,3},{5,4},{6,5},{7,6},{0,7},{9,8},{10,9},{11,1... | collective-permute-start | bytes 49544 | tf_op jit(solution)/shard_map/ppermute | solution.py:34
  347.0 2.8 copy.26
  349.9 3.0 convolution_bitcast_fusion
  354.5 4.7 %collective-permute-start.17 = (f32[1,258,1]{2,1,0:T(8,128)}, f32[1,258,1]{2,1,0:T(8,128)}, u32[]{:S(2)}, u32[]{:S(2)}) collective-permute-start(f32[1,258,1]{2,1,0:T(8,128)} %get-tuple-element.65), channel_id=1, source_target_pairs={{1,0},{2,1},{3,2},{4,3},{5,4},{6,5},{7,6},{0,7},{9,8},{10,9},{11,1... | collective-permute-start | bytes 3104 | tf_op jit(solution)/shard_map/ppermute | solution.py:34
  359.2 46.8 %fusion.12 = f32[16,256,512]{2,1,0:T(8,128)} fusion(f32[16,256,512]{2,1,0:T(8,128)} %fusion.27, f32[16,258,1]{2,1,0:T(8,128)} %copy.26, f32[16,1,512]{2,1,0:T(1,128)S(1)} %collective-permute-done.9, f32[16,1,512]{2,1,0:T(1,128)S(1)} %collective-permute-done.8, f32[16,258,1]{2,1,0:T(8,128)} %copy.24, f32[15,256,512]{2,1,0:T(8,128)} %fusion.36, ...), kind=kLoop, calls=%fused_computation.23 | loop fusion | flops 71303168 | bytes 52068616 | tf_op jit(solution)/shard_map/add | solution.py:181
  407.9 4.2 fusion.53
  414.2 11.6 %span_inverse.1 = f32[4,1024,512]{2,1,0:T(8,128)} custom-call(f32[4,4,512,256]{3,2,1,0:T(8,128)} %all-to-all-done.1.waves_ref, bf16[2,2,512,512]{3,2,1,0:T(8,128)(2,1)} %constant.131.clone.table_ref), custom_call_target="tpu_custom_call" | custom-call | flops 6442450944 | bytes 16777216 | tf_op jit(solution)/shard_map/span_inverse/pallas_call | solution.py:305
  (81 shorter events, 40.3 us)
Async XLA Ops:
  19.1 5.8 %copy-start.6 = (f32[2]{0:T(128)S(1)}, f32[2]{0:T(128)}, u32[]{:S(2)}) copy-start(f32[2]{0:T(128)} %param.19) | copy-start | bytes 28
  19.1 154.1 %all-to-all-start = ((f32[4,4,512,256]{3,2,1,0:T(8,128)}), f32[4,4,512,256]{3,2,1,0:T(8,128)}, u32[]{:S(2)}, u32[]{:S(2)}) async-start(f32[4,4,512,256]{3,2,1,0:T(8,128)} %span_forward.1), calls=%async_computation | async-start | bytes 16777216 | tf_op jit(solution)/shard_map/all_to_all | solution.py:244
  24.9 325.0 %all-gather.3.cloned.1.call-start = ((), (), s32[]{:S(2)}) async-start(), calls=%async_computation.2 | async-start | bytes 2621440 | tf_op jit(solution)/shard_map/all_gather | solution.py:336
  25.6 16.5 %copy-start.3 = (f32[256,512]{1,0:T(8,128)S(1)}, f32[256,512]{1,0:T(8,128)}, u32[]{:S(2)}) copy-start(f32[256,512]{1,0:T(8,128)} %param.17) | copy-start | bytes 1572868
  25.6 18.3 %copy-start.4 = (f32[8,4,16,256]{3,2,0,1:T(8,128)S(1)}, f32[8,4,16,256]{3,2,0,1:T(8,128)}, u32[]{:S(2)}) copy-start(f32[8,4,16,256]{3,2,0,1:T(8,128)} %constant.135.clone) | copy-start | bytes 1572868
  33.2 3.4 copy-start
  36.7 81.9 %collective-permute-start = (f32[16,1,512]{2,1,0:T(1,128)S(1)}, f32[16,1,512]{2,1,0:T(1,128)S(1)}, u32[]{:S(2)}, u32[]{:S(2)}) collective-permute-start(f32[16,1,512]{2,1,0:T(1,128)S(1)} %get-tuple-element.60), channel_id=1, source_target_pairs={{0,8},{8,16},{16,24},{24,0},{1,9},{9,17},{17,25},{25,1},{2,10},{10... | collective-permute-start | bytes 98312 | tf_op jit(solution)/shard_map/ppermute | solution.py:32
  37.2 81.4 %collective-permute-start.2 = (f32[16,1,512]{2,1,0:T(1,128)S(1)}, f32[16,1,512]{2,1,0:T(1,128)S(1)}, u32[]{:S(2)}, u32[]{:S(2)}) collective-permute-start(f32[16,1,512]{2,1,0:T(1,128)S(1)} %get-tuple-element.61), channel_id=1, source_target_pairs={{8,0},{16,8},{24,16},{0,24},{9,1},{17,9},{25,17},{1,25},{10,2},{18... | collective-permute-start | bytes 98312 | tf_op jit(solution)/shard_map/ppermute | solution.py:34
  40.3 88.6 %collective-permute-start.1 = (f32[16,1,512]{2,1,0:T(1,128)S(1)}, f32[16,1,512]{2,1,0:T(1,128)S(1)}, u32[]{:S(2)}, u32[]{:S(2)}) collective-permute-start(f32[16,1,512]{2,1,0:T(1,128)S(1)} %get-tuple-element.62), channel_id=1, source_target_pairs={{0,8},{8,16},{16,24},{24,0},{1,9},{9,17},{17,25},{25,1},{2,10},{10... | collective-permute-start | bytes 98312 | tf_op jit(solution)/shard_map/ppermute | solution.py:32
  40.9 91.1 %collective-permute-start.3 = (f32[16,1,512]{2,1,0:T(1,128)S(1)}, f32[16,1,512]{2,1,0:T(1,128)S(1)}, u32[]{:S(2)}, u32[]{:S(2)}) collective-permute-start(f32[16,1,512]{2,1,0:T(1,128)S(1)} %get-tuple-element.63), channel_id=1, source_target_pairs={{8,0},{16,8},{24,16},{0,24},{9,1},{17,9},{25,17},{1,25},{10,2},{18... | collective-permute-start | bytes 98312 | tf_op jit(solution)/shard_map/ppermute | solution.py:34
  43.2 96.5 %collective-permute-start.12 = (f32[1,1,512]{2,1,0:T(1,128)S(1)}, f32[1,1,512]{2,1,0:T(1,128)S(1)}, u32[]{:S(2)}, u32[]{:S(2)}) collective-permute-start(f32[1,1,512]{2,1,0:T(1,128)S(1)} %get-tuple-element.68), channel_id=1, source_target_pairs={{0,8},{8,16},{16,24},{24,0},{1,9},{9,17},{17,25},{25,1},{2,10},{10... | collective-permute-start | bytes 6152 | tf_op jit(solution)/shard_map/ppermute | solution.py:32
  118.6 25.9 %collective-permute-start.13 = (f32[1,1,512]{2,1,0:T(1,128)S(1)}, f32[1,1,512]{2,1,0:T(1,128)S(1)}, u32[]{:S(2)}, u32[]{:S(2)}) collective-permute-start(f32[1,1,512]{2,1,0:T(1,128)S(1)} %get-tuple-element.69), channel_id=1, source_target_pairs={{8,0},{16,8},{24,16},{0,24},{9,1},{17,9},{25,17},{1,25},{10,2},{18... | collective-permute-start | bytes 6152 | tf_op jit(solution)/shard_map/ppermute | solution.py:34
  125.4 19.9 %collective-permute-start.4 = (f32[16,258,1]{1,0,2:T(8,128)S(1)}, f32[16,258,1]{1,0,2:T(8,128)S(1)}, u32[]{:S(2)}, u32[]{:S(2)}) collective-permute-start(f32[16,258,1]{1,0,2:T(8,128)S(1)} %copy.15), channel_id=1, source_target_pairs={{0,1},{1,2},{2,3},{3,4},{4,5},{5,6},{6,7},{7,0},{8,9},{9,10},{10,1... | collective-permute-start | bytes 49544 | tf_op jit(solution)/shard_map/ppermute | solution.py:32
  128.9 21.8 %collective-permute-start.6 = (f32[16,258,1]{1,0,2:T(8,128)S(1)}, f32[16,258,1]{1,0,2:T(8,128)S(1)}, u32[]{:S(2)}, u32[]{:S(2)}) collective-permute-start(f32[16,258,1]{1,0,2:T(8,128)S(1)} %copy.19), channel_id=1, source_target_pairs={{1,0},{2,1},{3,2},{4,3},{5,4},{6,5},{7,6},{0,7},{9,8},{10,9},{11,1... | collective-permute-start | bytes 49544 | tf_op jit(solution)/shard_map/ppermute | solution.py:34
  138.8 14.0 %collective-permute-start.5 = (f32[16,258,1]{1,0,2:T(8,128)S(1)}, f32[16,258,1]{1,0,2:T(8,128)S(1)}, u32[]{:S(2)}, u32[]{:S(2)}) collective-permute-start(f32[16,258,1]{1,0,2:T(8,128)S(1)} %copy.17), channel_id=1, source_target_pairs={{0,1},{1,2},{2,3},{3,4},{4,5},{5,6},{6,7},{7,0},{8,9},{9,10},{10,1... | collective-permute-start | bytes 49544 | tf_op jit(solution)/shard_map/ppermute | solution.py:32
  139.8 15.1 %collective-permute-start.7 = (f32[16,258,1]{1,0,2:T(8,128)S(1)}, f32[16,258,1]{1,0,2:T(8,128)S(1)}, u32[]{:S(2)}, u32[]{:S(2)}) collective-permute-start(f32[16,258,1]{1,0,2:T(8,128)S(1)} %copy.21), channel_id=1, source_target_pairs={{1,0},{2,1},{3,2},{4,3},{5,4},{6,5},{7,6},{0,7},{9,8},{10,9},{11,1... | collective-permute-start | bytes 49544 | tf_op jit(solution)/shard_map/ppermute | solution.py:34
  145.3 260.8 %collective-permute-start.14 = (f32[1,258,1]{2,1,0:T(8,128)}, f32[1,258,1]{2,1,0:T(8,128)}, u32[]{:S(2)}, u32[]{:S(2)}) collective-permute-start(f32[1,258,1]{2,1,0:T(8,128)} %get-tuple-element.66), channel_id=1, source_target_pairs={{0,1},{1,2},{2,3},{3,4},{4,5},{5,6},{6,7},{7,0},{8,9},{9,10},{10,1... | collective-permute-start | bytes 3104 | tf_op jit(solution)/shard_map/ppermute | solution.py:32
  145.3 260.8 %collective-permute-start.15 = (f32[1,258,1]{2,1,0:T(8,128)}, f32[1,258,1]{2,1,0:T(8,128)}, u32[]{:S(2)}, u32[]{:S(2)}) collective-permute-start(f32[1,258,1]{2,1,0:T(8,128)} %get-tuple-element.67), channel_id=1, source_target_pairs={{1,0},{2,1},{3,2},{4,3},{5,4},{6,5},{7,6},{0,7},{9,8},{10,9},{11,1... | collective-permute-start | bytes 3104 | tf_op jit(solution)/shard_map/ppermute | solution.py:34
  173.3 24.0 %copy-start.5 = (f32[4,16,256]{2,0,1:T(4,128)S(1)}, f32[4,16,256]{2,0,1:T(4,128)}, u32[]{:S(2)}) copy-start(f32[4,16,256]{2,0,1:T(4,128)} %constant.134.clone) | copy-start | bytes 196612
  306.4 23.3 %collective-permute-start.8 = (f32[16,1,512]{2,1,0:T(1,128)S(1)}, f32[16,1,512]{2,1,0:T(1,128)S(1)}, u32[]{:S(2)}, u32[]{:S(2)}) collective-permute-start(f32[16,1,512]{2,1,0:T(1,128)S(1)} %get-tuple-element.58), channel_id=1, source_target_pairs={{0,8},{8,16},{16,24},{24,0},{1,9},{9,17},{17,25},{25,1},{2,10},{10... | collective-permute-start | bytes 98312 | tf_op jit(solution)/shard_map/ppermute | solution.py:32
  306.5 23.3 %collective-permute-start.9 = (f32[16,1,512]{2,1,0:T(1,128)S(1)}, f32[16,1,512]{2,1,0:T(1,128)S(1)}, u32[]{:S(2)}, u32[]{:S(2)}) collective-permute-start(f32[16,1,512]{2,1,0:T(1,128)S(1)} %get-tuple-element.59), channel_id=1, source_target_pairs={{8,0},{16,8},{24,16},{0,24},{9,1},{17,9},{25,17},{1,25},{10,2},{18... | collective-permute-start | bytes 98312 | tf_op jit(solution)/shard_map/ppermute | solution.py:34
  308.2 106.0 %all-to-all-start.1 = ((f32[4,4,512,256]{3,2,1,0:T(8,128)}), f32[4,4,512,256]{3,2,1,0:T(8,128)}, u32[]{:S(2)}, u32[]{:S(2)}) async-start(f32[4,4,512,256]{3,2,1,0:T(8,128)} %bitcast.226), calls=%async_computation.1 | async-start | bytes 16777216 | tf_op jit(solution)/shard_map/all_to_all | solution.py:298
  314.1 15.7 %copy-start.1 = (f32[16,256,512]{2,1,0:T(8,128)S(1)}, f32[16,256,512]{2,1,0:T(8,128)}, u32[]{:S(2)}) copy-start(f32[16,256,512]{2,1,0:T(8,128)} %fusion.27) | copy-start | bytes 25165828
  335.2 9.8 %collective-permute-start.10 = (f32[16,258,1]{1,0,2:T(8,128)S(1)}, f32[16,258,1]{1,0,2:T(8,128)S(1)}, u32[]{:S(2)}, u32[]{:S(2)}) collective-permute-start(f32[16,258,1]{1,0,2:T(8,128)S(1)} %copy.23), channel_id=1, source_target_pairs={{0,1},{1,2},{2,3},{3,4},{4,5},{5,6},{6,7},{7,0},{8,9},{9,10},{10,1... | collective-permute-start | bytes 49544 | tf_op jit(solution)/shard_map/ppermute | solution.py:32
  338.3 8.7 %collective-permute-start.11 = (f32[16,258,1]{1,0,2:T(8,128)}, f32[16,258,1]{1,0,2:T(8,128)}, u32[]{:S(2)}, u32[]{:S(2)}) collective-permute-start(f32[16,258,1]{1,0,2:T(8,128)} %copy.25), channel_id=1, source_target_pairs={{1,0},{2,1},{3,2},{4,3},{5,4},{6,5},{7,6},{0,7},{9,8},{10,9},{11,1... | collective-permute-start | bytes 49544 | tf_op jit(solution)/shard_map/ppermute | solution.py:34
  352.9 0.8 copy-start.2
  354.5 51.6 %collective-permute-start.16 = (f32[1,258,1]{2,1,0:T(8,128)}, f32[1,258,1]{2,1,0:T(8,128)}, u32[]{:S(2)}, u32[]{:S(2)}) collective-permute-start(f32[1,258,1]{2,1,0:T(8,128)} %get-tuple-element.64), channel_id=1, source_target_pairs={{0,1},{1,2},{2,3},{3,4},{4,5},{5,6},{6,7},{7,0},{8,9},{9,10},{10,1... | collective-permute-start | bytes 3104 | tf_op jit(solution)/shard_map/ppermute | solution.py:32
  354.5 51.6 %collective-permute-start.17 = (f32[1,258,1]{2,1,0:T(8,128)}, f32[1,258,1]{2,1,0:T(8,128)}, u32[]{:S(2)}, u32[]{:S(2)}) collective-permute-start(f32[1,258,1]{2,1,0:T(8,128)} %get-tuple-element.65), channel_id=1, source_target_pairs={{1,0},{2,1},{3,2},{4,3},{5,4},{6,5},{7,6},{0,7},{9,8},{10,9},{11,1... | collective-permute-start | bytes 3104 | tf_op jit(solution)/shard_map/ppermute | solution.py:34
Sparse Core Ops, SparseCore 0:
  258.8 19.0 all-gather.2

commit v2 on v1

--- a/solution.py
+++ b/solution.py
@@ -15,6 +15,8 @@
 STEP_RATE = 0.12
 LANES = 128
 SEGMENTS = 8
+ROWS = 8
+WIDTH = 2
 VMEM_BYTES = 56 * 2**20
 
 
@@ -22,20 +24,14 @@
     return pltpu.CompilerParams(vmem_limit_bytes=VMEM_BYTES)
 
 
-def with_halo(cells, sides, width):
-    for axis, dim in sides:
-        count = lax.axis_size(axis)
-        head = lax.slice_in_dim(cells, 0, width, axis=dim)
-        tail = lax.slice_in_dim(cells, cells.shape[dim] - width, cells.shape[dim], axis=dim)
-        cells = jnp.concatenate(
-            [
-                lax.ppermute(tail, axis, [(i, (i + 1) % count) for i in range(count)]),
-                cells,
-                lax.ppermute(head, axis, [((i + 1) % count, i) for i in range(count)]),
-            ],
-            axis=dim,
-        )
-    return cells
+def swap_edges(cells, axis, dim, width):
+    count = lax.axis_size(axis)
+    head = lax.slice_in_dim(cells, 0, width, axis=dim)
+    tail = lax.slice_in_dim(cells, cells.shape[dim] - width, cells.shape[dim], axis=dim)
+    return (
+        lax.ppermute(tail, axis, [(i, (i + 1) % count) for i in range(count)]),
+        lax.ppermute(head, axis, [((i + 1) % count, i) for i in range(count)]),
+    )
 
 
 def cas(product, length):
@@ -179,6 +175,127 @@
             - jnp.pad(vertical, ((1, 0), (0, 0), (0, 0)))
         )
     return centre_temp + STEP_RATE * net_flux
+
+
+def steps_kernel(
+    depth_len, cond_ref, temp_ref, phase_ref, above_t, above_c, below_t, below_c,
+    before_t, before_c, after_t, after_c, out_ref, temps, conds, nexts,
+):
+    step = pl.program_id(0)
+    rows, cols = out_ref.shape[1], out_ref.shape[2]
+    chunks = rows // ROWS
+    wide = cols + 2 * LANES
+
+    def conductance_step(plane, source, slots, chunk):
+        cond_slots = conds.shape[0]
+        upper = jnp.maximum(plane - 1, 0)
+        lower = jnp.minimum(plane + 1, depth_len - 1)
+
+        def get(ref, index, which):
+            start = pl.multiple_of(which * ROWS, ROWS)
+            return ref[index, pl.ds(start, ROWS), :]
+
+        row = lax.broadcasted_iota(jnp.int32, (ROWS, wide), 0)
+        prev = jnp.maximum(chunk - 1, 0)
+        after = jnp.minimum(chunk + 1, chunks + 1)
+
+        def around(ref, index):
+            here = get(ref, index, chunk)
+            up = jnp.where(
+                row == 0, pltpu.roll(get(ref, index, prev), 1, 0), pltpu.roll(here, 1, 0)
+            )
+            down = jnp.where(
+                row == ROWS - 1,
+                pltpu.roll(get(ref, index, after), ROWS - 1, 0),
+                pltpu.roll(here, ROWS - 1, 0),
+            )
+            return here, up, down
+
+        temp, temp_up, temp_down = around(source, plane % slots)
+        cond, cond_up, cond_down = around(conds, plane % cond_slots)
+        east = (cond + pltpu.roll(cond, wide - 1, 1)) * (pltpu.roll(temp, wide - 1, 1) - temp)
+        net = east - pltpu.roll(east, 1, 1)
+        net += (cond + cond_up) * (temp_up - temp) + (cond + cond_down) * (temp_down - temp)
+        for other in (upper, lower):
+            other_cond = get(conds, other % cond_slots, chunk)
+            net += (cond + other_cond) * (get(source, other % slots, chunk) - temp)
+        return temp + (0.5 * STEP_RATE) * net
+
+    @pl.when(step < depth_len)
+    def _():
+        def place(ref, slot, centre, above, below, before, after):
+            ref[slot, ROWS : ROWS + rows, LANES : LANES + cols] = centre
+            ref[slot, :ROWS, LANES : LANES + cols] = above[0]
+            ref[slot, ROWS + rows :, LANES : LANES + cols] = below[0]
+            ref[slot, :, :LANES] = before[0]
+            ref[slot, :, LANES + cols :] = after[0]
+
+        phases = jnp.where(phase_ref[0] == 1, cond_ref[1], cond_ref[0])
+        place(temps, step % 3, temp_ref[0], above_t, below_t, before_t, after_t)
+        place(conds, step % 4, phases, above_c, below_c, before_c, after_c)
+
+    @pl.when((step >= 1) & (step <= depth_len))
+    def _():
+        @pl.loop(0, chunks + 2)
+        def _(chunk):
+            start = pl.multiple_of(chunk * ROWS, ROWS)
+            nexts[(step - 1) % 3, pl.ds(start, ROWS), :] = conductance_step(
+                step - 1, temps, 3, chunk
+            )
+
+    @pl.when(step >= 2)
+    def _():
+        @pl.loop(0, chunks)
+        def _(chunk):
+            start = pl.multiple_of(chunk * ROWS, ROWS)
+            result = conductance_step(step - 2, nexts, 3, chunk + 1)
+            out_ref[0, pl.ds(start, ROWS), :] = result[:, LANES : LANES + cols]
+
+
+def two_steps(solid_temp, phase_map, phase_conductivity, above, below, before, after):
+    depth_len, rows, cols = solid_temp.shape
+    tall, wide = rows + 2 * ROWS, cols + 2 * LANES
+    before = jnp.pad(before, ((0, 0), (0, 0), (LANES - WIDTH, 0)))
+    after = jnp.pad(after, ((0, 0), (0, 0), (0, LANES - WIDTH)))
+
+    def spec(*shape, offset=0):
+        return pl.BlockSpec(
+            (1,) + shape, lambda i: (jnp.minimum(i, depth_len - 1) + offset, 0, 0)
+        )
+
+    def pair(*shape):
+        return [spec(*shape), spec(*shape, offset=depth_len)]
+
+    return pl.pallas_call(
+        functools.partial(steps_kernel, depth_len),
+        grid=(depth_len + 2,),
+        in_specs=[
+            pl.BlockSpec(memory_space=pltpu.SMEM),
+            spec(rows, cols),
+            spec(rows, cols),
+            *pair(ROWS, cols),
+            *pair(ROWS, cols),
+            *pair(tall, LANES),
+            *pair(tall, LANES),
+        ],
+        out_specs=pl.BlockSpec((1, rows, cols), lambda i: (jnp.maximum(i - 2, 0), 0, 0)),
+        out_shape=jax.ShapeDtypeStruct((depth_len, rows, cols), jnp.float32),
+        scratch_shapes=[
+            pltpu.VMEM((3, tall, wide), jnp.float32),
+            pltpu.VMEM((4, tall, wide), jnp.float32),
+            pltpu.VMEM((3, tall, wide), jnp.float32),
+        ],
+        compiler_params=params(),
+        cost_estimate=pl.CostEstimate(
+            flops=60 * depth_len * rows * cols,
+            bytes_accessed=16 * depth_len * rows * cols,
+            transcendentals=0,
+        ),
+        name="conduct_twice",
+    )(
+        phase_conductivity, solid_temp, phase_map,
+        above, above, below, below, before, before, after, after,
+    )
 
 
 def per_device(pressure_source, solid_temp, gas_wall_temp, phase_map, phase_conductivity):
@@ -223,6 +340,25 @@
     reach_right = lax.dynamic_slice_in_dim(
         jnp.concatenate([reach_loc, reach_loc]), (2 * pencils - 1 - pencil_idx) % pencils, pencils, 0
     )
+
+    tile_rows = span_len // groups
+
+    def conductivity(phases):
+        return jnp.where(phases == 1, phase_conductivity[1], phase_conductivity[0])
+
+    solid_len = solid_temp.shape[0]
+    edge_rows = [
+        jnp.concatenate([solid_temp[:, part], conductivity(phase_map[:, part]), gas_wall_temp[None, part]])
+        for part in (slice(0, ROWS), slice(tile_rows - ROWS, tile_rows))
+    ]
+    above, below = swap_edges(jnp.concatenate(edge_rows, axis=1), "grp", 1, ROWS)
+    edge_cols = []
+    for part in (slice(0, WIDTH), slice(stream_loc - WIDTH, stream_loc)):
+        inner = jnp.concatenate(
+            [solid_temp[:, :, part], conductivity(phase_map[:, :, part]), gas_wall_temp[None, :, part]]
+        )
+        edge_cols.append(jnp.concatenate([above[:, :, part], inner, below[:, :, part]], axis=1))
+    before, after = swap_edges(jnp.concatenate(edge_cols, axis=2), "pen", 2, WIDTH)
 
     spectral = pl.pallas_call(
         span_forward_kernel,
@@ -241,6 +377,20 @@
         ),
         name="span_forward",
     )(pressure_source, table_parts)
+    spectral, above, below, before, after = lax.optimization_barrier(
+        (spectral, above, below, before, after)
+    )
+    unheated = two_steps(
+        solid_temp, phase_map, phase_conductivity, above, below, before, after
+    )
+
+    def top_plane(inner, plane):
+        rows = jnp.concatenate([above[plane, -1:], inner, below[plane, :1]])
+        span = slice(ROWS - 1, ROWS + tile_rows + 1)
+        return jnp.concatenate([before[plane, span, -1:], rows, after[plane, span, :1]], axis=1)
+
+    top_cond = top_plane(conductivity(phase_map[0]), solid_len)
+    dry_flux = top_plane(gas_wall_temp, 2 * solid_len) - top_plane(solid_temp[0], 0)
     moved = lax.all_to_all(spectral, "grp", split_axis=0, concat_axis=0, tiled=True)
     moved = moved.reshape(depth_len, stream_loc, waves_loc)
 
@@ -320,14 +470,6 @@
         name="span_inverse",
     )(returned, table_parts)
 
-    tile_rows = span_len // groups
-    sides = (("grp", 1), ("pen", 2))
-    cell_cond = jnp.where(phase_map == 1, phase_conductivity[1], phase_conductivity[0])
-    padded_temp, padded_cond = with_halo(solid_temp, sides, 1), with_halo(cell_cond, sides, 1)
-    first_temp = conduct(padded_temp, padded_cond)
-    unheated = conduct(with_halo(first_temp, sides, 1), padded_cond)
-    dry_flux = with_halo((gas_wall_temp - solid_temp[0])[None], sides, 1)
-
     span_rows = np.arange(-1, span_len + 1) % span_len
     wall_table = cas(span_rows[:, None] * order.reshape(1, -1), span_len)
     wall_rows = lax.dynamic_slice_in_dim(
@@ -341,11 +483,12 @@
         precision=HIGH,
         preferred_element_type=f32,
     )
-    wall = with_halo(wall[None], (("pen", 2),), 1)
-    flux = HEAT_TRANSFER * (dry_flux + PRESSURE_WORK * wall)
+    wall_left, wall_right = swap_edges(wall, "pen", 1, 1)
+    wall = jnp.concatenate([wall_left, wall, wall_right], axis=1)
+    flux = (HEAT_TRANSFER * (dry_flux + PRESSURE_WORK * wall))[None]
     centre_flux = flux[0, 1:-1, 1:-1]
-    between = 0.5 * (padded_cond[0] + padded_cond[1])[1:-1, 1:-1] * centre_flux
-    lateral = conduct(flux, padded_cond[:1])[0]
+    between = 0.5 * (top_cond[1:-1, 1:-1] + conductivity(phase_map[1])) * centre_flux
+    lateral = conduct(flux, top_cond[None])[0]
     top = STEP_RATE * (centre_flux + lateral - STEP_RATE * between)
     second = STEP_RATE * STEP_RATE * between
     final_temp = unheated.at[0].add(top).at[1].add(second)

time: 434 us -> 487 us (1.12)
  Pallas kernels: 68.9 us -> 243 us
  other arithmetic: 178 us -> 23.4 us
  waiting for transfers between devices: 54.9 us -> 99.9 us
  starting transfers between devices: 43 us -> 24.1 us
  local copies, waits for them, and re-layouts: 40 us -> 47.3 us
    pallas_call x0 -> x1, Pallas kernels: none -> 174 us  [two_steps(): pl.pallas_call(functools.partial(steps_kernel, depth_len), grid=(depth_le...]
    add x4 -> x1, other arithmetic: 97.1 us -> 0.71 us  [per_device(): flux = (HEAT_TRANSFER * (dry_flux + PRESSURE_WORK * wall))[None]]
    all_to_all x1, waiting for transfers between devices: 0.01 us -> 90.1 us  [per_device(): lax.all_to_all(spectral, 'grp', split_axis=0, concat_axis=0, tiled=True)]
    ppermute x18 -> x6, waiting for transfers between devices: 54.9 us -> 0.02 us  [the longest x3 0.01 us: swap_edges(): lax.ppermute(tail, axis, [(i, (i + 1) % count) for i in range(count)])]
    mul x2 -> x0, other arithmetic: 31.2 us -> none  [conduct(): 0.5 * (centre_cond[1:] + centre_cond[:-1])]
    ppermute x18 -> x6, starting transfers between devices: 31.4 us -> 12.6 us  [the longest x3 8.32 us: swap_edges(): lax.ppermute(head, axis, [((i + 1) % count, i) for i in range(count)])]
    concatenate x1 -> x6, other arithmetic: 16.3 us -> 2.26 us  [the longest x2 1.7 us: per_device(): jnp.concatenate([solid_temp[:, part], conductivity(phase_map[:, part]), g...]
    slice x4 -> x0, other arithmetic: 12.3 us -> none  [with_halo(): lax.slice_in_dim(cells, cells.shape[dim] - width, cells.shape[dim], axis=...]
  transfers between devices with their start and end apart: 21 -> 9, of which waited for: 1 -> 2; matrix products, arithmetic and copies ran while one was open for 50% -> 12% of each run, Pallas kernels for 10% -> 38%
where the time goes in v2:
time: 487 us; the launch traced here: 486 us
  Pallas kernels  243 us (50%)
  waiting for transfers between devices  99.9 us (21%)
  local copies, waits for them, and re-layouts  47.3 us (10%)
  blocking collectives  30.7 us (6%)
  starting transfers between devices  24.1 us (5%)
  other arithmetic  23.4 us (5%)
  between operations  14.5 us (3%)
    pallas_call x1, Pallas kernels, two_steps(): pl.pallas_call(functools.partial(steps_kernel, depth_len), grid=(depth_le...  174 us
    all_to_all x1, waiting for transfers between devices, per_device(): lax.all_to_all(spectral, 'grp', split_axis=0, concat_axis=0, tiled=True)  90.1 us
    all_gather x1, blocking collectives, per_device(): gathered = lax.all_gather(jnp.stack([tail_all, head_all]), 'pen')  30.7 us
    pallas_call x1, Pallas kernels, per_device(): pl.pallas_call(lambda s, r, m, h, t: ends_kernel(vectors, s, FirstRow(r),...  24 us
    pallas_call x1, Pallas kernels, per_device(): pl.pallas_call(lambda m, r, g, a, b, o, c: solve_kernel(vectors, m, First...  21.3 us
    pallas_call x1, Pallas kernels, per_device(): pl.pallas_call(span_forward_kernel, grid=(depth_loc,), in_specs=[pl.Block...  12 us
    pallas_call x1, Pallas kernels, per_device(): pl.pallas_call(span_inverse_kernel, grid=(depth_loc,), in_specs=[pl.Block...  11.6 us
  transfers between devices with their start and end apart: 9, of which 2 were waited for; matrix products, arithmetic and copies ran while one was open for 12% of the time, Pallas kernels for 38%

profile of v2, /device:TPU:0, one launch (start us, length us, event | category | flops | bytes accessed | tf_op | source)
XLA Modules:
  0.0 485.9 jit_solution(10525690774448402889)
XLA Ops:
  9.3 2.6 fusion.23
  14.0 2.0 collective-permute-start.1
  16.0 4.3 fusion.81
  20.2 2.8 fusion.80
  23.2 2.2 copy.53
  26.7 2.2 copy.52
  29.6 2.2 copy.55
  34.2 2.3 collective-permute-start.2
  37.3 3.1 collective-permute-start.3
  40.4 12.0 %span_forward.1 = f32[4,4,512,256]{3,2,1,0:T(8,128)} custom-call(f32[4,1024,512]{2,1,0:T(8,128)} %source_ref.1, bf16[2,2,512,512]{3,2,1,0:T(8,128)(2,1)} %constant.130.clone.table_ref), custom_call_target="tpu_custom_call" | custom-call | flops 6442450944 | bytes 16777216 | tf_op jit(solution)/shard_map/span_forward/pallas_call | solution.py:363
  53.0 5.7 %all-to-all-start = ((f32[4,4,512,256]{3,2,1,0:T(8,128)}), f32[4,4,512,256]{3,2,1,0:T(8,128)}, u32[]{:S(2)}, u32[]{:S(2)}) async-start(f32[4,4,512,256]{3,2,1,0:T(8,128)} %span_forward.1), calls=%async_computation | async-start | bytes 16777216 | tf_op jit(solution)/shard_map/all_to_all | solution.py:394
  61.8 90.1 %all-to-all-done = f32[4,4,512,256]{3,2,1,0:T(8,128)} async-done(((f32[4,4,512,256]{3,2,1,0:T(8,128)}), f32[4,4,512,256]{3,2,1,0:T(8,128)}, u32[]{:S(2)}, u32[]{:S(2)}) %all-to-all-start) | async-done | bytes 8388640 | tf_op jit(solution)/shard_map/all_to_all | solution.py:394
  151.9 24.0 %stream_ends.1 = (f32[16,64,8,256]{3,2,1,0:T(8,128)}, f32[16,8,256]{2,1,0:T(8,128)}, f32[16,8,256]{2,1,0:T(8,128)}) custom-call(f32[16,512,256]{2,1,0:T(8,128)} %bitcast.6.s, f32[16,1,256]{2,1,0:T(1,128)} %dynamic-slice_bitcast_fusion.5.r), custom_call_target="tpu_custom_call" | custom-call | flops 67108864 | bytes 16777216 | tf_op jit(solution)/shard_map/stream_ends/pallas_call | solution.py:411
  175.9 2.4 fusion.63
  178.3 30.7 %all-gather = f32[16,16,256]{2,1,0:T(8,128)S(1)} all-gather(f32[2,16,256]{2,1,0:T(8,128)S(1)} %copy.42), channel_id=2, replica_groups=mesh['grp'=4,'pen'=8] {'pen'}, dimensions={0}, use_global_device_ids=true | all-gather | bytes 294912 | tf_op jit(solution)/shard_map/all_gather | solution.py:430
  209.1 2.2 fusion.59
  213.0 21.3 %stream_solve.1 = f32[16,512,256]{2,1,0:T(8,128)} custom-call(f32[16,64,8,256]{3,2,1,0:T(8,128)} %get-tuple-element.35.m, f32[16,1,256]{2,1,0:T(1,128)} %dynamic-slice_bitcast_fusion.5.r, f32[16,1,256]{2,1,0:T(1,128)} %dynamic-slice_bitcast_fusion.4.g, f32[16,8,256]{2,1,0:T(8,128)} %stack.10.a, f32[16,8,256]{2,1,0:T(8,128)} %stack.11.b), custom_call_target="tpu_custom_call" | custom-call | flops 67108864 | bytes 16777216 | tf_op jit(solution)/shard_map/stream_solve/pallas_call | solution.py:436
  234.4 5.7 %all-to-all-start.1 = ((f32[4,4,512,256]{3,2,1,0:T(8,128)}), f32[4,4,512,256]{3,2,1,0:T(8,128)}, u32[]{:S(2)}, u32[]{:S(2)}) async-start(f32[4,4,512,256]{3,2,1,0:T(8,128)} %bitcast.222), calls=%async_computation.1 | async-start | bytes 16777216 | tf_op jit(solution)/shard_map/all_to_all | solution.py:448
  240.3 1.9 slice.357
  244.1 2.4 select_bitcast_fusion
  246.5 1.9 slice_bitcast_fusion
  248.4 3.0 copy.43
  252.4 3.0 copy.44
  256.3 5.9 %pad.12.before_t.before_c = f32[33,272,128]{2,1,0:T(8,128)} pad(f32[33,272,2]{2,1,0:T(8,128)} %copy.43, f32[]{:T(128)} %constant.123.clone.1), padding=0_0x0_0x126_0 | pad | bytes 4667524 | tf_op jit(solution)/shard_map/jit(_pad)/pad | solution.py:258
  262.3 2.4 pad.13.after_t.after_c
  265.9 9.7 %all-gather.3.cloned.1.call-done = f32[4,512,256]{2,1,0:T(8,128)} async-done(((f32[1,512,256]{2,1,0:T(8,128)}), f32[4,512,256]{2,1,0:T(8,128)}) %all-gather.3.cloned.1.call-update) | async-done | bytes 2097168 | tf_op jit(solution)/shard_map/all_gather | solution.py:478
  275.6 2.7 fusion
  280.5 3.3 collective-permute-start.5
  283.8 174.5 %conduct_twice.1 = f32[16,256,512]{2,1,0:T(8,128)} custom-call(f32[2]{0:T(128)} %cond_ref.1, f32[16,256,512]{2,1,0:T(8,128)} %temp_ref.1, s32[16,256,512]{2,1,0:T(8,128)} %phase_ref.1, f32[33,8,512]{2,1,0:T(8,128)} %copy-done.1, f32[33,8,512]{2,1,0:T(8,128)} %copy-done.1, f32[33,8,512]{2,1,0:T(8,128)} %copy-done.2, f32[33,8,512]{2,1,0:T(8,128)} %copy-done.2, ...), custom_call_target="tpu_custom_call" | custom-call | flops 125829120 | bytes 33554432 | tf_op jit(solution)/shard_map/conduct_twice/pallas_call | solution.py:269
  459.6 4.5 fusion.8
  464.0 3.5 fusion.9
  467.5 11.6 %span_inverse.1 = f32[4,1024,512]{2,1,0:T(8,128)} custom-call(f32[4,4,512,256]{3,2,1,0:T(8,128)} %all-to-all-done.1.waves_ref, bf16[2,2,512,512]{3,2,1,0:T(8,128)(2,1)} %constant.130.clone.table_ref), custom_call_target="tpu_custom_call" | custom-call | flops 6442450944 | bytes 16777216 | tf_op jit(solution)/shard_map/span_inverse/pallas_call | solution.py:455
  (92 shorter events, 23.5 us)
Async XLA Ops:
  12.7 20.5 %collective-permute-start = (f32[33,8,512]{2,1,0:T(8,128)}, f32[33,8,512]{2,1,0:T(8,128)S(1)}, u32[]{:S(2)}, u32[]{:S(2)}) collective-permute-start(f32[33,8,512]{2,1,0:T(8,128)} %pad_maximum_fusion), channel_id=1, source_target_pairs={{0,8},{8,16},{16,24},{24,0},{1,9},{9,17},{17,25},{25,1},{2,10},{10... | collective-permute-start | bytes 1622024 | tf_op jit(solution)/shard_map/ppermute | solution.py:32
  13.2 7.1 %copy-start = (f32[16,256,512]{2,1,0:T(8,128)S(1)}, f32[16,256,512]{2,1,0:T(8,128)}, u32[]{:S(2)}) copy-start(f32[16,256,512]{2,1,0:T(8,128)} %temp_ref.1) | copy-start | bytes 25165828
  14.0 19.5 %collective-permute-start.1 = (f32[33,8,512]{2,1,0:T(8,128)}, f32[33,8,512]{2,1,0:T(8,128)S(1)}, u32[]{:S(2)}, u32[]{:S(2)}) collective-permute-start(f32[33,8,512]{2,1,0:T(8,128)} %pad_maximum_fusion.1), channel_id=1, source_target_pairs={{8,0},{16,8},{24,16},{0,24},{9,1},{17,9},{25,17},{1,25},{10,2},{18... | collective-permute-start | bytes 1622024 | tf_op jit(solution)/shard_map/ppermute | solution.py:33
  20.2 2.8 copy-start.4
  33.2 231.4 %copy-start.1 = (f32[33,8,512]{2,1,0:T(8,128)}, f32[33,8,512]{2,1,0:T(8,128)S(1)}, u32[]{:S(2)}) copy-start(f32[33,8,512]{2,1,0:T(8,128)S(1)} %collective-permute-done.above_t.above_c) | copy-start | bytes 1622020
  33.6 18.8 %copy-start.2 = (f32[33,8,512]{2,1,0:T(8,128)}, f32[33,8,512]{2,1,0:T(8,128)S(1)}, u32[]{:S(2)}) copy-start(f32[33,8,512]{2,1,0:T(8,128)S(1)} %collective-permute-done.1.below_t.below_c) | copy-start | bytes 1622020
  34.2 18.2 %collective-permute-start.2 = (f32[33,272,2]{1,2,0:T(2,128)S(1)}, f32[33,272,2]{1,2,0:T(2,128)S(1)}, u32[]{:S(2)}, u32[]{:S(2)}) collective-permute-start(f32[33,272,2]{1,2,0:T(2,128)S(1)} %pad_maximum_fusion.2), channel_id=1, source_target_pairs={{0,1},{1,2},{2,3},{3,4},{4,5},{5,6},{6,7},{7,0},{8,9},{9,10},{10,1... | collective-permute-start | bytes 215432 | tf_op jit(solution)/shard_map/ppermute | solution.py:32
  37.3 15.1 %collective-permute-start.3 = (f32[33,272,2]{1,2,0:T(2,128)S(1)}, f32[33,272,2]{1,2,0:T(2,128)S(1)}, u32[]{:S(2)}, u32[]{:S(2)}) collective-permute-start(f32[33,272,2]{1,2,0:T(2,128)S(1)} %pad_maximum_fusion.3), channel_id=1, source_target_pairs={{1,0},{2,1},{3,2},{4,3},{5,4},{6,5},{7,6},{0,7},{9,8},{10,9},{11,1... | collective-permute-start | bytes 215432 | tf_op jit(solution)/shard_map/ppermute | solution.py:33
  52.3 6.4 %copy-start.8 = (f32[8,4,16,256]{3,2,0,1:T(8,128)S(1)}, f32[8,4,16,256]{3,2,0,1:T(8,128)}, u32[]{:S(2)}) copy-start(f32[8,4,16,256]{3,2,0,1:T(8,128)} %constant.134.clone) | copy-start | bytes 1572868
  52.3 0.6 copy-start.9
  52.4 0.7 copy-start.11
  53.0 98.8 %all-to-all-start = ((f32[4,4,512,256]{3,2,1,0:T(8,128)}), f32[4,4,512,256]{3,2,1,0:T(8,128)}, u32[]{:S(2)}, u32[]{:S(2)}) async-start(f32[4,4,512,256]{3,2,1,0:T(8,128)} %span_forward.1), calls=%async_computation | async-start | bytes 16777216 | tf_op jit(solution)/shard_map/all_to_all | solution.py:394
  58.8 117.1 %copy-start.13 = (f32[4,16,256]{2,0,1:T(4,128)S(1)}, f32[4,16,256]{2,0,1:T(4,128)}, u32[]{:S(2)}) copy-start(f32[4,16,256]{2,0,1:T(4,128)} %constant.133.clone) | copy-start | bytes 196612
  234.4 233.2 %all-to-all-start.1 = ((f32[4,4,512,256]{3,2,1,0:T(8,128)}), f32[4,4,512,256]{3,2,1,0:T(8,128)}, u32[]{:S(2)}, u32[]{:S(2)}) async-start(f32[4,4,512,256]{3,2,1,0:T(8,128)} %bitcast.222), calls=%async_computation.1 | async-start | bytes 16777216 | tf_op jit(solution)/shard_map/all_to_all | solution.py:448
  240.0 8.4 %copy-start.10 = (f32[33,272,2]{1,2,0:T(2,128)S(1)}, f32[33,272,2]{1,2,0:T(2,128)}, u32[]{:S(2)}) copy-start(f32[33,272,2]{1,2,0:T(2,128)} %copy-done.9) | copy-start | bytes 215428
  240.1 35.5 %all-gather.3.cloned.1.call-start = ((), (), s32[]{:S(2)}) async-start(), calls=%async_computation.2 | async-start | bytes 2621440 | tf_op jit(solution)/shard_map/all_gather | solution.py:478
  243.6 8.8 %copy-start.12 = (f32[33,272,2]{1,2,0:T(2,128)S(1)}, f32[33,272,2]{1,2,0:T(2,128)}, u32[]{:S(2)}) copy-start(f32[33,272,2]{1,2,0:T(2,128)} %copy-done.11) | copy-start | bytes 215428
  255.5 6.7 %slice-start = ((s8[4595712]{0:T(1024)(128)(4,1)}), s8[401408]{0:T(1024)(128)(4,1)S(1)}, s32[]{:S(2)}) async-start(s8[4595712]{0:T(1024)(128)(4,1)} %bitcast.223), calls=%async_computation.3 | async-start | bytes 802816
  256.3 5.9 %slice-start.1 = ((s8[4595712]{0:T(1024)(128)(4,1)}), s8[4194304]{0:T(1024)(128)(4,1)S(1)}, s32[]{:S(2)}) async-start(s8[4595712]{0:T(1024)(128)(4,1)} %bitcast.223), calls=%async_computation.4 | async-start | bytes 8388608
  262.2 3.2 copy-start.5
  262.2 3.2 copy-start.3
  262.2 3.3 copy-start.6
  262.2 3.3 copy-start.7
  279.0 179.8 %collective-permute-start.4 = (f32[258,1]{1,0:T(8,128)}, f32[258,1]{1,0:T(8,128)S(1)}, u32[]{:S(2)}, u32[]{:S(2)}) collective-permute-start(f32[258,1]{1,0:T(8,128)} %get-tuple-element.74), channel_id=1, source_target_pairs={{0,1},{1,2},{2,3},{3,4},{4,5},{5,6},{6,7},{7,0},{8,9},{9,10},{10,1... | collective-permute-start | bytes 3104 | tf_op jit(solution)/shard_map/ppermute | solution.py:32
  280.5 178.4 %collective-permute-start.5 = (f32[258,1]{1,0:T(8,128)S(1)}, f32[258,1]{1,0:T(8,128)S(1)}, u32[]{:S(2)}, u32[]{:S(2)}) collective-permute-start(f32[258,1]{1,0:T(8,128)S(1)} %get-tuple-element.75), channel_id=1, source_target_pairs={{1,0},{2,1},{3,2},{4,3},{5,4},{6,5},{7,6},{0,7},{9,8},{10,9},{11,1... | collective-permute-start | bytes 3104 | tf_op jit(solution)/shard_map/ppermute | solution.py:33
Sparse Core Ops, SparseCore 0:
  242.5 33.0 all-gather.2

commit v3 on v2

--- a/solution.py
+++ b/solution.py
@@ -67,7 +67,7 @@
 
 def span_forward_kernel(source_ref, table_ref, out_ref):
     half = table_ref.shape[2]
-    width = out_ref.shape[3]
+    lots, width = out_ref.shape[0], out_ref.shape[4]
     head = source_ref[0, :half]
     tail = source_ref[0, half:]
     for parity in range(2):
@@ -76,16 +76,20 @@
         result = dot_split(folded, table, ((0,), (0,)))
         per = half // width
         for part in range(per):
-            out_ref[parity * per + part, 0] = result[:, part * width : (part + 1) * width]
-
-
-def span_inverse_kernel(waves_ref, table_ref, out_ref):
+            group = parity * (per // lots) + part // lots
+            out_ref[part % lots, group, 0] = result[:, part * width : (part + 1) * width]
+
+
+def span_inverse_kernel(*refs):
+    waves_refs, table_ref, out_ref = refs[:-2], refs[-2], refs[-1]
     half = table_ref.shape[2]
-    per = waves_ref.shape[0] // 2
+    per = waves_refs[0].shape[0] // 2
     halves = []
     for parity in range(2):
         table = (table_ref[parity, 0], table_ref[parity, 1])
-        waves = jnp.concatenate([waves_ref[parity * per + part, 0] for part in range(per)], axis=1)
+        waves = jnp.concatenate(
+            [ref[parity * per + part, 0] for part in range(per) for ref in waves_refs], axis=1
+        )
         halves.append(dot_split(table, split(waves), ((1,), (1,))))
     out_ref[0, :half] = halves[0] + halves[1]
     out_ref[0, half:] = halves[0] - halves[1]
@@ -179,37 +183,31 @@
 
 def steps_kernel(
     depth_len, cond_ref, temp_ref, phase_ref, above_t, above_c, below_t, below_c,
-    before_t, before_c, after_t, after_c, out_ref, temps, conds, nexts,
+    side_t, side_c, out_ref, temps, conds, nexts,
 ):
     step = pl.program_id(0)
     rows, cols = out_ref.shape[1], out_ref.shape[2]
     chunks = rows // ROWS
-    wide = cols + 2 * LANES
+    wide = cols + LANES
 
     def conductance_step(plane, source, slots, chunk):
         cond_slots = conds.shape[0]
         upper = jnp.maximum(plane - 1, 0)
         lower = jnp.minimum(plane + 1, depth_len - 1)
 
-        def get(ref, index, which):
-            start = pl.multiple_of(which * ROWS, ROWS)
-            return ref[index, pl.ds(start, ROWS), :]
-
-        row = lax.broadcasted_iota(jnp.int32, (ROWS, wide), 0)
-        prev = jnp.maximum(chunk - 1, 0)
-        after = jnp.minimum(chunk + 1, chunks + 1)
+        start = pl.multiple_of(chunk * ROWS, ROWS)
+        tall = 2 * ROWS
+
+        def get(ref, index):
+            return ref[index, pl.ds(start + ROWS, tall), :]
 
         def around(ref, index):
-            here = get(ref, index, chunk)
-            up = jnp.where(
-                row == 0, pltpu.roll(get(ref, index, prev), 1, 0), pltpu.roll(here, 1, 0)
+            window = ref[index, pl.ds(start, tall + 2 * ROWS), :]
+            return (
+                window[ROWS : ROWS + tall],
+                window[ROWS - 1 : ROWS - 1 + tall],
+                window[ROWS + 1 : ROWS + 1 + tall],
             )
-            down = jnp.where(
-                row == ROWS - 1,
-                pltpu.roll(get(ref, index, after), ROWS - 1, 0),
-                pltpu.roll(here, ROWS - 1, 0),
-            )
-            return here, up, down
 
         temp, temp_up, temp_down = around(source, plane % slots)
         cond, cond_up, cond_down = around(conds, plane % cond_slots)
@@ -217,46 +215,45 @@
         net = east - pltpu.roll(east, 1, 1)
         net += (cond + cond_up) * (temp_up - temp) + (cond + cond_down) * (temp_down - temp)
         for other in (upper, lower):
-            other_cond = get(conds, other % cond_slots, chunk)
-            net += (cond + other_cond) * (get(source, other % slots, chunk) - temp)
+            other_cond = get(conds, other % cond_slots)
+            net += (cond + other_cond) * (get(source, other % slots) - temp)
         return temp + (0.5 * STEP_RATE) * net
 
     @pl.when(step < depth_len)
     def _():
-        def place(ref, slot, centre, above, below, before, after):
-            ref[slot, ROWS : ROWS + rows, LANES : LANES + cols] = centre
-            ref[slot, :ROWS, LANES : LANES + cols] = above[0]
-            ref[slot, ROWS + rows :, LANES : LANES + cols] = below[0]
-            ref[slot, :, :LANES] = before[0]
-            ref[slot, :, LANES + cols :] = after[0]
+        def place(ref, slot, centre, above, below, side):
+            ref[slot, 2 * ROWS : 2 * ROWS + rows, :cols] = centre
+            ref[slot, ROWS : 2 * ROWS, :cols] = above[0]
+            ref[slot, 2 * ROWS + rows : 3 * ROWS + rows, :cols] = below[0]
+            ref[slot, ROWS : 3 * ROWS + rows, cols:] = side[0]
 
         phases = jnp.where(phase_ref[0] == 1, cond_ref[1], cond_ref[0])
-        place(temps, step % 3, temp_ref[0], above_t, below_t, before_t, after_t)
-        place(conds, step % 4, phases, above_c, below_c, before_c, after_c)
+        place(temps, step % 3, temp_ref[0], above_t, below_t, side_t)
+        place(conds, step % 4, phases, above_c, below_c, side_c)
 
     @pl.when((step >= 1) & (step <= depth_len))
     def _():
-        @pl.loop(0, chunks + 2)
-        def _(chunk):
-            start = pl.multiple_of(chunk * ROWS, ROWS)
-            nexts[(step - 1) % 3, pl.ds(start, ROWS), :] = conductance_step(
-                step - 1, temps, 3, chunk
+        @pl.loop(0, (chunks + 2) // 2)
+        def _(pair):
+            start = pl.multiple_of(2 * pair * ROWS, ROWS) + ROWS
+            nexts[(step - 1) % 3, pl.ds(start, 2 * ROWS), :] = conductance_step(
+                step - 1, temps, 3, 2 * pair
             )
 
     @pl.when(step >= 2)
     def _():
-        @pl.loop(0, chunks)
-        def _(chunk):
-            start = pl.multiple_of(chunk * ROWS, ROWS)
-            result = conductance_step(step - 2, nexts, 3, chunk + 1)
-            out_ref[0, pl.ds(start, ROWS), :] = result[:, LANES : LANES + cols]
+        @pl.loop(0, chunks // 2)
+        def _(pair):
+            start = pl.multiple_of(2 * pair * ROWS, ROWS)
+            result = conductance_step(step - 2, nexts, 3, 2 * pair + 1)
+            out_ref[0, pl.ds(start, 2 * ROWS), :] = result[:, :cols]
 
 
 def two_steps(solid_temp, phase_map, phase_conductivity, above, below, before, after):
     depth_len, rows, cols = solid_temp.shape
-    tall, wide = rows + 2 * ROWS, cols + 2 * LANES
-    before = jnp.pad(before, ((0, 0), (0, 0), (LANES - WIDTH, 0)))
-    after = jnp.pad(after, ((0, 0), (0, 0), (0, LANES - WIDTH)))
+    tall, wide = rows + 2 * ROWS, cols + LANES
+    gap = jnp.zeros(before.shape[:2] + (LANES - 2 * WIDTH,), jnp.float32)
+    side = jnp.concatenate([after, gap, before], axis=2)
 
     def spec(*shape, offset=0):
         return pl.BlockSpec(
@@ -276,14 +273,13 @@
             *pair(ROWS, cols),
             *pair(ROWS, cols),
             *pair(tall, LANES),
-            *pair(tall, LANES),
         ],
         out_specs=pl.BlockSpec((1, rows, cols), lambda i: (jnp.maximum(i - 2, 0), 0, 0)),
         out_shape=jax.ShapeDtypeStruct((depth_len, rows, cols), jnp.float32),
         scratch_shapes=[
-            pltpu.VMEM((3, tall, wide), jnp.float32),
-            pltpu.VMEM((4, tall, wide), jnp.float32),
-            pltpu.VMEM((3, tall, wide), jnp.float32),
+            pltpu.VMEM((3, tall + 2 * ROWS, wide), jnp.float32),
+            pltpu.VMEM((4, tall + 2 * ROWS, wide), jnp.float32),
+            pltpu.VMEM((3, tall + 2 * ROWS, wide), jnp.float32),
         ],
         compiler_params=params(),
         cost_estimate=pl.CostEstimate(
@@ -294,7 +290,7 @@
         name="conduct_twice",
     )(
         phase_conductivity, solid_temp, phase_map,
-        above, above, below, below, before, before, after, after,
+        above, above, below, below, side, side,
     )
 
 
@@ -310,6 +306,8 @@
     waves_loc = span_len // groups
     steps = stream_loc // SEGMENTS
     f32 = jnp.float32
+
+    lots = waves_loc // LANES
 
     order = wave_order(span_len, groups)
     row = np.arange(half)
@@ -367,8 +365,8 @@
             pl.BlockSpec((1, span_len, stream_loc), lambda z: (z, 0, 0)),
             pl.BlockSpec((2, 2, half, half), lambda z: (0, 0, 0, 0)),
         ],
-        out_specs=pl.BlockSpec((groups, 1, stream_loc, waves_loc), lambda z: (0, z, 0, 0)),
-        out_shape=jax.ShapeDtypeStruct((groups, depth_loc, stream_loc, waves_loc), f32),
+        out_specs=pl.BlockSpec((lots, groups, 1, stream_loc, LANES), lambda z: (0, 0, z, 0, 0)),
+        out_shape=jax.ShapeDtypeStruct((lots, groups, depth_loc, stream_loc, LANES), f32),
         compiler_params=params(),
         cost_estimate=pl.CostEstimate(
             flops=6 * depth_loc * stream_loc * span_len * half,
@@ -377,9 +375,6 @@
         ),
         name="span_forward",
     )(pressure_source, table_parts)
-    spectral, above, below, before, after = lax.optimization_barrier(
-        (spectral, above, below, before, after)
-    )
     unheated = two_steps(
         solid_temp, phase_map, phase_conductivity, above, below, before, after
     )
@@ -391,14 +386,11 @@
 
     top_cond = top_plane(conductivity(phase_map[0]), solid_len)
     dry_flux = top_plane(gas_wall_temp, 2 * solid_len) - top_plane(solid_temp[0], 0)
-    moved = lax.all_to_all(spectral, "grp", split_axis=0, concat_axis=0, tiled=True)
-    moved = moved.reshape(depth_len, stream_loc, waves_loc)
-
     data_spec = pl.BlockSpec((depth_len, stream_loc, LANES), lambda w: (0, 0, w))
     mode_spec = pl.BlockSpec((depth_len, steps, SEGMENTS, LANES), lambda w: (0, 0, 0, w))
     wave_spec = pl.BlockSpec((depth_len, 1, LANES), lambda w: (0, 0, w))
     ends_spec = pl.BlockSpec((depth_len, SEGMENTS, LANES), lambda w: (0, 0, w))
-    ends_shape = jax.ShapeDtypeStruct((depth_len, SEGMENTS, waves_loc), f32)
+    ends_shape = jax.ShapeDtypeStruct((depth_len, SEGMENTS, LANES), f32)
     cost = pl.CostEstimate(
         flops=2 * depth_len**2 * stream_loc * waves_loc,
         bytes_accessed=8 * depth_len * stream_loc * waves_loc,
@@ -408,55 +400,67 @@
     def rowed(value):
         return value[:, None, :]
 
-    modes, heads, tails = pl.pallas_call(
-        lambda s, r, m, h, t: ends_kernel(vectors, s, FirstRow(r), m, h, t),
-        grid=(waves_loc // LANES,),
-        in_specs=[data_spec, wave_spec],
-        out_specs=[mode_spec, ends_spec, ends_spec],
-        out_shape=[
-            jax.ShapeDtypeStruct((depth_len, steps, SEGMENTS, waves_loc), f32),
-            ends_shape,
-            ends_shape,
-        ],
-        compiler_params=params(),
-        cost_estimate=cost,
-        name="stream_ends",
-    )(moved, rowed(root_loc))
-    tail_all = tails[:, 0]
-    head_all = heads[:, SEGMENTS - 1]
-    for part in range(1, SEGMENTS):
-        tail_all = tails[:, part] + hop_loc * tail_all
-        head_all = heads[:, SEGMENTS - 1 - part] + hop_loc * head_all
-    gathered = lax.all_gather(jnp.stack([tail_all, head_all]), "pen")
-    left = [jnp.sum(reach_left * gathered[:, 0], axis=0)]
-    right = [jnp.sum(reach_right * gathered[:, 1], axis=0)]
-    for part in range(SEGMENTS - 1):
-        left.append(tails[:, part] + hop_loc * left[-1])
-        right.append(heads[:, SEGMENTS - 1 - part] + hop_loc * right[-1])
-    solved = pl.pallas_call(
-        lambda m, r, g, a, b, o, c: solve_kernel(vectors, m, FirstRow(r), FirstRow(g), a, b, o, c),
-        grid=(waves_loc // LANES,),
-        in_specs=[mode_spec, wave_spec, wave_spec, ends_spec, ends_spec],
-        out_specs=data_spec,
-        out_shape=jax.ShapeDtypeStruct((depth_len, stream_loc, waves_loc), f32),
-        scratch_shapes=[pltpu.VMEM((depth_len, steps, SEGMENTS, LANES), f32)],
-        compiler_params=params(),
-        cost_estimate=cost,
-        name="stream_solve",
-    )(modes, rowed(root_loc), rowed(gain_loc), jnp.stack(left, 1), jnp.stack(right[::-1], 1))
-
-    returned = lax.all_to_all(
-        solved.reshape(groups, depth_loc, stream_loc, waves_loc),
-        "grp",
-        split_axis=0,
-        concat_axis=0,
-        tiled=True,
-    )
+    def lot_of(value, lot):
+        return value[..., lot * LANES : (lot + 1) * LANES]
+
+    solved_top, returned = [], []
+    for lot in range(lots):
+        roots, gains, hops = (lot_of(value, lot) for value in (root_loc, gain_loc, hop_loc))
+        lefts, rights = lot_of(reach_left, lot), lot_of(reach_right, lot)
+        moved = lax.all_to_all(spectral[lot], "grp", split_axis=0, concat_axis=0, tiled=True)
+        moved = moved.reshape(depth_len, stream_loc, LANES)
+        modes, heads, tails = pl.pallas_call(
+            lambda s, r, m, h, t: ends_kernel(vectors, s, FirstRow(r), m, h, t),
+            grid=(1,),
+            in_specs=[data_spec, wave_spec],
+            out_specs=[mode_spec, ends_spec, ends_spec],
+            out_shape=[
+                jax.ShapeDtypeStruct((depth_len, steps, SEGMENTS, LANES), f32),
+                ends_shape,
+                ends_shape,
+            ],
+            compiler_params=params(),
+            cost_estimate=cost,
+            name="stream_ends",
+        )(moved, rowed(roots))
+        tail_all = tails[:, 0]
+        head_all = heads[:, SEGMENTS - 1]
+        for part in range(1, SEGMENTS):
+            tail_all = tails[:, part] + hops * tail_all
+            head_all = heads[:, SEGMENTS - 1 - part] + hops * head_all
+        gathered = lax.all_gather(jnp.stack([tail_all, head_all]), "pen")
+        left = [jnp.sum(lefts * gathered[:, 0], axis=0)]
+        right = [jnp.sum(rights * gathered[:, 1], axis=0)]
+        for part in range(SEGMENTS - 1):
+            left.append(tails[:, part] + hops * left[-1])
+            right.append(heads[:, SEGMENTS - 1 - part] + hops * right[-1])
+        solved = pl.pallas_call(
+            lambda m, r, g, a, b, o, c: solve_kernel(vectors, m, FirstRow(r), FirstRow(g), a, b, o, c),
+            grid=(1,),
+            in_specs=[mode_spec, wave_spec, wave_spec, ends_spec, ends_spec],
+            out_specs=data_spec,
+            out_shape=jax.ShapeDtypeStruct((depth_len, stream_loc, LANES), f32),
+            scratch_shapes=[pltpu.VMEM((depth_len, steps, SEGMENTS, LANES), f32)],
+            compiler_params=params(),
+            cost_estimate=cost,
+            name="stream_solve",
+        )(modes, rowed(roots), rowed(gains), jnp.stack(left, 1), jnp.stack(right[::-1], 1))
+
+        back = lax.all_to_all(
+            solved.reshape(groups, depth_loc, stream_loc, LANES),
+            "grp",
+            split_axis=0,
+            concat_axis=0,
+            tiled=True,
+        )
+        solved_top.append(solved[0])
+        returned.append(back)
+
     pressure = pl.pallas_call(
         span_inverse_kernel,
         grid=(depth_loc,),
         in_specs=[
-            pl.BlockSpec((groups, 1, stream_loc, waves_loc), lambda z: (0, z, 0, 0)),
+            *[pl.BlockSpec((groups, 1, stream_loc, LANES), lambda z: (0, z, 0, 0))] * lots,
             pl.BlockSpec((2, 2, half, half), lambda z: (0, 0, 0, 0)),
         ],
         out_specs=pl.BlockSpec((1, span_len, stream_loc), lambda z: (z, 0, 0)),
@@ -468,14 +472,14 @@
             transcendentals=0,
         ),
         name="span_inverse",
-    )(returned, table_parts)
+    )(*returned, table_parts)
 
     span_rows = np.arange(-1, span_len + 1) % span_len
     wall_table = cas(span_rows[:, None] * order.reshape(1, -1), span_len)
     wall_rows = lax.dynamic_slice_in_dim(
         jnp.asarray(wall_table, f32), group_idx * tile_rows, tile_rows + 2, 0
     )
-    wall_waves = lax.all_gather(solved[0], "grp")
+    wall_waves = lax.all_gather(jnp.concatenate(solved_top, axis=1), "grp")
     wall = jnp.einsum(
         "ygk,gxk->yx",
         wall_rows.reshape(tile_rows + 2, groups, waves_loc),

time: 487 us -> 456 us (0.936)
  Pallas kernels: 243 us -> 173 us
  blocking collectives: 30.7 us -> 62.1 us
  waiting for transfers between devices: 99.9 us -> 85.1 us
  local copies, waits for them, and re-layouts: 47.3 us -> 56.1 us
  starting transfers between devices: 24.1 us -> 31.3 us
  other arithmetic: 23.4 us -> 29.6 us
    pallas_call x1, Pallas kernels: 174 us -> 96.1 us  [two_steps(): pl.pallas_call(functools.partial(steps_kernel, depth_len), grid=(depth_le...]
    all_gather x1 -> x2, blocking collectives: 30.7 us -> 62.1 us  [per_device(): gathered = lax.all_gather(jnp.stack([tail_all, head_all]), 'pen')]
    all_gather x1, waiting for transfers between devices: 9.73 us -> 0.02 us  [per_device(): wall_waves = lax.all_gather(jnp.concatenate(solved_top, axis=1), 'grp')]
    squeeze x0 -> x3, local copies, waits for them, and re-layouts: none -> 9.66 us  [the longest x1 7.72 us: per_device(): spectral[lot]]
    all_to_all x2 -> x4, starting transfers between devices: 11.3 us -> 19.7 us  [the longest x2 10 us: per_device(): lax.all_to_all(spectral[lot], 'grp', split_axis=0, concat_axis=0, tiled=T...]
    pad x2 -> x0, local copies, waits for them, and re-layouts: 8.29 us -> none  [the longest x1 5.91 us: two_steps(): before = jnp.pad(before, ((0, 0), (0, 0), (LANES - WIDTH, 0)))]
    concatenate x0 -> x3, other arithmetic: none -> 8.03 us  [the longest x1 7.06 us: two_steps(): side = jnp.concatenate([after, gap, before], axis=2)]
    ppermute x0 -> x2, local copies, waits for them, and re-layouts: none -> 6.11 us  [the longest x1 3.06 us: swap_edges(): lax.ppermute(head, axis, [((i + 1) % count, i) for i in range(count)])]
  transfers between devices with their start and end apart: 9 -> 11, of which waited for: 2 -> 2; matrix products, arithmetic and copies ran while one was open for 12% -> 16% of each run, Pallas kernels for 38% -> 35%
where the time goes in v3:
time: 456 us; the launch traced here: 455 us
  Pallas kernels  173 us (38%)
  waiting for transfers between devices  85.1 us (19%)
  blocking collectives  62.1 us (14%)
  local copies, waits for them, and re-layouts  56.1 us (12%)
  starting transfers between devices  31.3 us (7%)
  other arithmetic  29.6 us (6%)
  between operations  14.5 us (3%)
    pallas_call x1, Pallas kernels, two_steps(): pl.pallas_call(functools.partial(steps_kernel, depth_len), grid=(depth_le...  96.1 us
    all_gather x2, blocking collectives, per_device(): gathered = lax.all_gather(jnp.stack([tail_all, head_all]), 'pen')  62.1 us
    all_to_all x2, waiting for transfers between devices, per_device(): lax.all_to_all(spectral[lot], 'grp', split_axis=0, concat_axis=0, tiled=T...  45.6 us
    all_to_all x2, waiting for transfers between devices, per_device(): lax.all_to_all(solved.reshape(groups, depth_loc, stream_loc, LANES), 'grp...  39.5 us
    pallas_call x2, Pallas kernels, per_device(): pl.pallas_call(lambda s, r, m, h, t: ends_kernel(vectors, s, FirstRow(r),...  28.1 us
    pallas_call x2, Pallas kernels, per_device(): pl.pallas_call(lambda m, r, g, a, b, o, c: solve_kernel(vectors, m, First...  25.7 us
    pallas_call x1, Pallas kernels, per_device(): pl.pallas_call(span_forward_kernel, grid=(depth_loc,), in_specs=[pl.Block...  12 us
    pallas_call x1, Pallas kernels, per_device(): pl.pallas_call(span_inverse_kernel, grid=(depth_loc,), in_specs=[*[pl.Blo...  11.5 us
  transfers between devices with their start and end apart: 11, of which 2 were waited for; matrix products, arithmetic and copies ran while one was open for 16% of the time, Pallas kernels for 35%

profile of v3, /device:TPU:0, one launch (start us, length us, event | category | flops | bytes accessed | tf_op | source)
XLA Modules:
  0.0 454.7 jit_solution(18106412014425863679)
XLA Ops:
  7.2 12.0 %span_forward.1 = f32[2,4,4,512,128]{4,3,2,1,0:T(8,128)} custom-call(f32[4,1024,512]{2,1,0:T(8,128)} %source_ref.1, bf16[2,2,512,512]{3,2,1,0:T(8,128)(2,1)} %constant.130.clone.table_ref.refs_2_), custom_call_target="tpu_custom_call" | custom-call | flops 6442450944 | bytes 16777216 | tf_op jit(solution)/shard_map/span_forward/pallas_call | solution.py:361
  19.1 7.7 %slice_bitcast_fusion = (f32[4,4,512,128]{3,2,1,0:T(8,128)}, f32[4,4,512,128]{3,2,1,0:T(8,128)}) fusion(f32[2,4,4,512,128]{4,3,2,1,0:T(8,128)} %span_forward.1), kind=kLoop, calls=%fused_computation.1 | loop fusion | bytes 16777216 | tf_op jit(solution)/shard_map/squeeze | solution.py:410
  26.9 5.0 %all-to-all-start = ((f32[4,4,512,128]{3,2,1,0:T(8,128)}), f32[4,4,512,128]{3,2,1,0:T(8,128)}, u32[]{:S(2)}, u32[]{:S(2)}) async-start(f32[4,4,512,128]{3,2,1,0:T(8,128)} %get-tuple-element.76), calls=%async_computation | async-start | bytes 8388608 | tf_op jit(solution)/shard_map/all_to_all | solution.py:410
  32.5 2.7 fusion.23
  35.2 45.6 %all-to-all-done = f32[4,4,512,128]{3,2,1,0:T(8,128)} async-done(((f32[4,4,512,128]{3,2,1,0:T(8,128)}), f32[4,4,512,128]{3,2,1,0:T(8,128)}, u32[]{:S(2)}, u32[]{:S(2)}) %all-to-all-start) | async-done | bytes 4194336 | tf_op jit(solution)/shard_map/all_to_all | solution.py:410
  80.8 5.0 %all-to-all-start.2 = ((f32[4,4,512,128]{3,2,1,0:T(8,128)}), f32[4,4,512,128]{3,2,1,0:T(8,128)}, u32[]{:S(2)}, u32[]{:S(2)}) async-start(f32[4,4,512,128]{3,2,1,0:T(8,128)} %get-tuple-element.75), calls=%async_computation.2 | async-start | bytes 8388608 | tf_op jit(solution)/shard_map/all_to_all | solution.py:410
  90.2 4.3 fusion.45
  94.5 2.2 copy.244
  101.8 1.9 slice_bitcast_fusion.2
  103.7 4.3 fusion.44
  107.9 14.0 %stream_ends.2 = (f32[16,64,8,128]{3,2,1,0:T(8,128)}, f32[16,8,128]{2,1,0:T(8,128)}, f32[16,8,128]{2,1,0:T(8,128)}) custom-call(f32[16,512,128]{2,1,0:T(8,128)} %bitcast.1.s, f32[16,1,128]{2,1,0:T(1,128)} %bitcast.443), custom_call_target="tpu_custom_call" | custom-call | flops 67108864 | bytes 16777216 | tf_op jit(solution)/shard_map/stream_ends/pallas_call | solution.py:412
  123.7 31.6 %all-gather = f32[16,16,128]{2,1,0:T(8,128)S(1)} all-gather(f32[2,16,128]{2,1,0:T(8,128)S(1)} %pad_maximum_fusion.6), channel_id=2, replica_groups=mesh['grp'=4,'pen'=8] {'pen'}, dimensions={0}, use_global_device_ids=true | all-gather | bytes 147456 | tf_op jit(solution)/shard_map/all_gather | solution.py:431
  155.4 14.0 %stream_ends.3 = (f32[16,64,8,128]{3,2,1,0:T(8,128)}, f32[16,8,128]{2,1,0:T(8,128)}, f32[16,8,128]{2,1,0:T(8,128)}) custom-call(f32[16,512,128]{2,1,0:T(8,128)} %bitcast.52.s, f32[16,1,128]{2,1,0:T(1,128)} %bitcast.445), custom_call_target="tpu_custom_call" | custom-call | flops 67108864 | bytes 16777216 | tf_op jit(solution)/shard_map/stream_ends/pallas_call | solution.py:412
  171.2 30.5 %all-gather.1 = f32[16,16,128]{2,1,0:T(8,128)S(1)} all-gather(f32[2,16,128]{2,1,0:T(8,128)S(1)} %pad_maximum_fusion.7), channel_id=3, replica_groups=mesh['grp'=4,'pen'=8] {'pen'}, dimensions={0}, use_global_device_ids=true | all-gather | bytes 147456 | tf_op jit(solution)/shard_map/all_gather | solution.py:431
  203.3 12.8 %stream_solve.3 = f32[16,512,128]{2,1,0:T(8,128)} custom-call(f32[16,64,8,128]{3,2,1,0:T(8,128)} %get-tuple-element.35.m, f32[16,1,128]{2,1,0:T(1,128)} %bitcast.446, f32[16,1,128]{2,1,0:T(1,128)} %bitcast.455, f32[16,8,128]{2,1,0:T(8,128)} %copy.218.a, f32[16,8,128]{2,1,0:T(8,128)} %stack.167.b), custom_call_target="tpu_custom_call" | custom-call | flops 67108864 | bytes 16777216 | tf_op jit(solution)/shard_map/stream_solve/pallas_call | solution.py:437
  216.0 4.9 %all-to-all-start.3 = ((f32[4,4,512,128]{3,2,1,0:T(8,128)}), f32[4,4,512,128]{3,2,1,0:T(8,128)}, u32[]{:S(2)}, u32[]{:S(2)}) async-start(f32[4,4,512,128]{3,2,1,0:T(8,128)} %bitcast.434), calls=%async_computation.3 | async-start | bytes 8388608 | tf_op jit(solution)/shard_map/all_to_all | solution.py:449
  222.4 12.9 %stream_solve.2 = f32[16,512,128]{2,1,0:T(8,128)} custom-call(f32[16,64,8,128]{3,2,1,0:T(8,128)} %get-tuple-element.32.m, f32[16,1,128]{2,1,0:T(1,128)} %bitcast.444, f32[16,1,128]{2,1,0:T(1,128)} %bitcast.454, f32[16,8,128]{2,1,0:T(8,128)} %copy.191.a, f32[16,8,128]{2,1,0:T(8,128)} %copy.192.b), custom_call_target="tpu_custom_call" | custom-call | flops 67108864 | bytes 16777216 | tf_op jit(solution)/shard_map/stream_solve/pallas_call | solution.py:437
  240.9 39.5 %all-to-all-done.3.refs_1_ = f32[4,4,512,128]{3,2,1,0:T(8,128)} async-done(((f32[4,4,512,128]{3,2,1,0:T(8,128)}), f32[4,4,512,128]{3,2,1,0:T(8,128)}, u32[]{:S(2)}, u32[]{:S(2)}) %all-to-all-start.3) | async-done | bytes 4194336 | tf_op jit(solution)/shard_map/all_to_all | solution.py:449
  280.4 4.8 %all-to-all-start.1 = ((f32[4,4,512,128]{3,2,1,0:T(8,128)}), f32[4,4,512,128]{3,2,1,0:T(8,128)}, u32[]{:S(2)}, u32[]{:S(2)}) async-start(f32[4,4,512,128]{3,2,1,0:T(8,128)} %bitcast.433), calls=%async_computation.1 | async-start | bytes 8388608 | tf_op jit(solution)/shard_map/all_to_all | solution.py:449
  285.2 2.4 constant_dynamic-slice_fusion
  289.4 2.2 copy.243
  292.5 2.5 select_bitcast_fusion
  300.3 3.5 collective-permute-start.2
  310.2 3.1 copy.229
  313.3 3.0 copy.230
  316.3 7.1 %pad_maximum_fusion.side_t.side_c = f32[33,272,128]{2,1,0:T(8,128)} fusion(f32[33,272,2]{2,1,0:T(8,128)} %copy.230, f32[33,272,2]{2,1,0:T(8,128)} %copy.229, f32[128]{0:T(128)S(1)} %pad.27.clone), kind=kLoop, calls=%fused_computation | loop fusion | flops 2297856 | bytes 4739840 | tf_op jit(solution)/shard_map/concatenate | solution.py:256
  323.4 96.1 %conduct_twice.1 = f32[16,256,512]{2,1,0:T(8,128)} custom-call(f32[2]{0:T(128)} %cond_ref.1, f32[16,256,512]{2,1,0:T(8,128)} %temp_ref.1, s32[16,256,512]{2,1,0:T(8,128)} %phase_ref.1, f32[33,8,512]{2,1,0:T(8,128)} %collective-permute-done.above_t.above_c, f32[33,8,512]{2,1,0:T(8,128)} %collective-permute-done.above_t.above_c, ...), custom_call_target="tpu_custom_call" | custom-call | flops 125829120 | bytes 33554432 | tf_op jit(solution)/shard_map/conduct_twice/pallas_call | solution.py:266
  419.8 2.7 fusion
  422.7 4.7 %collective-permute-start.5 = (f32[258,1]{1,0:T(8,128)S(1)}, f32[258,1]{1,0:T(8,128)S(1)}, u32[]{:S(2)}, u32[]{:S(2)}) collective-permute-start(f32[258,1]{1,0:T(8,128)S(1)} %get-tuple-element.84), channel_id=1, source_target_pairs={{1,0},{2,1},{3,2},{4,3},{5,4},{6,5},{7,6},{0,7},{9,8},{10,9},{11,1... | collective-permute-start | bytes 3104 | tf_op jit(solution)/shard_map/ppermute | solution.py:33
  427.3 11.5 %span_inverse.1 = f32[4,1024,512]{2,1,0:T(8,128)} custom-call(f32[4,4,512,128]{3,2,1,0:T(8,128)} %all-to-all-done.1.refs_0_, f32[4,4,512,128]{3,2,1,0:T(8,128)} %all-to-all-done.3.refs_1_, bf16[2,2,512,512]{3,2,1,0:T(8,128)(2,1)} %constant.130.clone.table_ref.refs_2_), custom_call_target="tpu_custom_call" | custom-call | flops 6442450944 | bytes 16777216 | tf_op jit(solution)/shard_map/span_inverse/pallas_call | solution.py:459
  439.6 4.6 %fusion.8 = f32[16,256,512]{2,1,0:T(8,128)} fusion(f32[16,256,512]{2,1,0:T(8,128)} %conduct_twice.1, f32[1,258,514]{2,1,0:T(8,128)S(1)} %fusion.2, f32[1,258,514]{2,1,0:T(8,128)S(1)} %maximum_bitcast_fusion, s32[16,256,512]{2,1,0:T(8,128)} %phase_ref.1, pred[1,256,512]{2,1,0:T(8,128)(4,1)S(1)} %get-tuple-element.43, f32[]{:T(128)} %bitcast.101, f32[]{:T(128)} %bitcast.100), kind=kLoop, calls=%fused_computation.21 | loop fusion | flops 4194304 | bytes 6947840 | tf_op jit(solution)/shard_map/scatter-add | solution.py:498
  444.2 3.6 fusion.9
  (114 shorter events, 37.6 us)
Async XLA Ops:
  26.9 5.0 %copy-start.7 = (f32[2]{0:T(128)S(1)}, f32[2]{0:T(128)}, u32[]{:S(2)}) copy-start(f32[2]{0:T(128)} %cond_ref.1) | copy-start | bytes 28
  26.9 53.9 %all-to-all-start = ((f32[4,4,512,128]{3,2,1,0:T(8,128)}), f32[4,4,512,128]{3,2,1,0:T(8,128)}, u32[]{:S(2)}, u32[]{:S(2)}) async-start(f32[4,4,512,128]{3,2,1,0:T(8,128)} %get-tuple-element.76), calls=%async_computation | async-start | bytes 8388608 | tf_op jit(solution)/shard_map/all_to_all | solution.py:410
  80.8 5.0 %copy-start.2 = (f32[256,512]{1,0:T(8,128)S(1)}, f32[256,512]{1,0:T(8,128)}, u32[]{:S(2)}) copy-start(f32[256,512]{1,0:T(8,128)} %param.17) | copy-start | bytes 1572868
  80.8 74.6 %all-to-all-start.2 = ((f32[4,4,512,128]{3,2,1,0:T(8,128)}), f32[4,4,512,128]{3,2,1,0:T(8,128)}, u32[]{:S(2)}, u32[]{:S(2)}) async-start(f32[4,4,512,128]{3,2,1,0:T(8,128)} %get-tuple-element.75), calls=%async_computation.2 | async-start | bytes 8388608 | tf_op jit(solution)/shard_map/all_to_all | solution.py:410
  86.7 208.4 %collective-permute-start = (f32[33,8,512]{2,1,0:T(8,128)}, f32[33,8,512]{2,1,0:T(8,128)}, u32[]{:S(2)}, u32[]{:S(2)}) collective-permute-start(f32[33,8,512]{2,1,0:T(8,128)} %pad_maximum_fusion.1), channel_id=1, source_target_pairs={{0,8},{8,16},{16,24},{24,0},{1,9},{9,17},{17,25},{25,1},{2,10},{10... | collective-permute-start | bytes 1622024 | tf_op jit(solution)/shard_map/ppermute | solution.py:32
  88.0 208.4 %collective-permute-start.1 = (f32[33,8,512]{2,1,0:T(8,128)}, f32[33,8,512]{2,1,0:T(8,128)}, u32[]{:S(2)}, u32[]{:S(2)}) collective-permute-start(f32[33,8,512]{2,1,0:T(8,128)} %pad_maximum_fusion.2), channel_id=1, source_target_pairs={{8,0},{16,8},{24,16},{0,24},{9,1},{17,9},{25,17},{1,25},{10,2},{18... | collective-permute-start | bytes 1622024 | tf_op jit(solution)/shard_map/ppermute | solution.py:33
  216.0 64.3 %all-to-all-start.3 = ((f32[4,4,512,128]{3,2,1,0:T(8,128)}), f32[4,4,512,128]{3,2,1,0:T(8,128)}, u32[]{:S(2)}, u32[]{:S(2)}) async-start(f32[4,4,512,128]{3,2,1,0:T(8,128)} %bitcast.434), calls=%async_computation.3 | async-start | bytes 8388608 | tf_op jit(solution)/shard_map/all_to_all | solution.py:449
  220.9 198.8 %all-gather.5.cloned.1.call-start = ((), (), s32[]{:S(2)}) async-start(), calls=%async_computation.4 | async-start | bytes 2621440 | tf_op jit(solution)/shard_map/all_gather | solution.py:482
  280.4 147.0 %all-to-all-start.1 = ((f32[4,4,512,128]{3,2,1,0:T(8,128)}), f32[4,4,512,128]{3,2,1,0:T(8,128)}, u32[]{:S(2)}, u32[]{:S(2)}) async-start(f32[4,4,512,128]{3,2,1,0:T(8,128)} %bitcast.433), calls=%async_computation.1 | async-start | bytes 8388608 | tf_op jit(solution)/shard_map/all_to_all | solution.py:449
  292.3 14.0 %copy-start.1 = (f32[256,512]{1,0:T(8,128)S(1)}, f32[256,512]{1,0:T(8,128)}, u32[]{:S(2)}) copy-start(f32[256,512]{1,0:T(8,128)} %slice_bitcast_fusion.2) | copy-start | bytes 1572868
  298.0 9.3 %collective-permute-start.3 = (f32[33,272,2]{1,2,0:T(2,128)S(1)}, f32[33,272,2]{1,2,0:T(2,128)S(1)}, u32[]{:S(2)}, u32[]{:S(2)}) collective-permute-start(f32[33,272,2]{1,2,0:T(2,128)S(1)} %pad_maximum_fusion.5), channel_id=1, source_target_pairs={{0,1},{1,2},{2,3},{3,4},{4,5},{5,6},{6,7},{7,0},{8,9},{9,10},{10,1... | collective-permute-start | bytes 215432 | tf_op jit(solution)/shard_map/ppermute | solution.py:32
  300.3 7.8 %collective-permute-start.2 = (f32[33,272,2]{1,2,0:T(2,128)S(1)}, f32[33,272,2]{1,2,0:T(2,128)S(1)}, u32[]{:S(2)}, u32[]{:S(2)}) collective-permute-start(f32[33,272,2]{1,2,0:T(2,128)S(1)} %pad_maximum_fusion.4), channel_id=1, source_target_pairs={{1,0},{2,1},{3,2},{4,3},{5,4},{6,5},{7,6},{0,7},{9,8},{10,9},{11,1... | collective-permute-start | bytes 215432 | tf_op jit(solution)/shard_map/ppermute | solution.py:33
  307.3 0.6 copy-start.5
  307.9 5.4 %copy-start.6 = (f32[33,272,2]{1,2,0:T(2,128)S(1)}, f32[33,272,2]{1,2,0:T(2,128)}, u32[]{:S(2)}) copy-start(f32[33,272,2]{1,2,0:T(2,128)} %copy-done.5) | copy-start | bytes 215428
  422.6 16.3 %collective-permute-start.4 = (f32[258,1]{1,0:T(8,128)S(1)}, f32[258,1]{1,0:T(8,128)S(1)}, u32[]{:S(2)}, u32[]{:S(2)}) collective-permute-start(f32[258,1]{1,0:T(8,128)S(1)} %get-tuple-element.83), channel_id=1, source_target_pairs={{0,1},{1,2},{2,3},{3,4},{4,5},{5,6},{6,7},{7,0},{8,9},{9,10},{10,1... | collective-permute-start | bytes 3104 | tf_op jit(solution)/shard_map/ppermute | solution.py:32
  422.6 16.2 %copy-start = (f32[1,258,512]{2,1,0:T(8,128)S(1)}, f32[1,258,512]{2,1,0:T(8,128)}, u32[]{:S(2)}) copy-start(f32[1,258,512]{2,1,0:T(8,128)} %maximum_bitcast_fusion.2) | copy-start | bytes 1585156
  422.6 16.2 %copy-start.3 = (f32[1,258,1]{2,1,0:T(8,128)S(1)}, f32[1,258,1]{2,1,0:T(8,128)}, u32[]{:S(2)}) copy-start(f32[1,258,1]{2,1,0:T(8,128)} %copy.233) | copy-start | bytes 3100
  422.6 16.2 %copy-start.4 = (f32[1,258,1]{2,1,0:T(8,128)S(1)}, f32[1,258,1]{2,1,0:T(8,128)}, u32[]{:S(2)}) copy-start(f32[1,258,1]{2,1,0:T(8,128)} %copy.234) | copy-start | bytes 3100
  422.7 16.2 %collective-permute-start.5 = (f32[258,1]{1,0:T(8,128)S(1)}, f32[258,1]{1,0:T(8,128)S(1)}, u32[]{:S(2)}, u32[]{:S(2)}) collective-permute-start(f32[258,1]{1,0:T(8,128)S(1)} %get-tuple-element.84), channel_id=1, source_target_pairs={{1,0},{2,1},{3,2},{4,3},{5,4},{6,5},{7,6},{0,7},{9,8},{10,9},{11,1... | collective-permute-start | bytes 3104 | tf_op jit(solution)/shard_map/ppermute | solution.py:33
Sparse Core Ops, SparseCore 0:
  238.2 35.3 all-gather.4

commit v4 on v2

--- a/solution.py
+++ b/solution.py
@@ -179,37 +179,31 @@
 
 def steps_kernel(
     depth_len, cond_ref, temp_ref, phase_ref, above_t, above_c, below_t, below_c,
-    before_t, before_c, after_t, after_c, out_ref, temps, conds, nexts,
+    side_t, side_c, out_ref, temps, conds, nexts,
 ):
     step = pl.program_id(0)
     rows, cols = out_ref.shape[1], out_ref.shape[2]
     chunks = rows // ROWS
-    wide = cols + 2 * LANES
+    wide = cols + LANES
 
     def conductance_step(plane, source, slots, chunk):
         cond_slots = conds.shape[0]
         upper = jnp.maximum(plane - 1, 0)
         lower = jnp.minimum(plane + 1, depth_len - 1)
 
-        def get(ref, index, which):
-            start = pl.multiple_of(which * ROWS, ROWS)
-            return ref[index, pl.ds(start, ROWS), :]
-
-        row = lax.broadcasted_iota(jnp.int32, (ROWS, wide), 0)
-        prev = jnp.maximum(chunk - 1, 0)
-        after = jnp.minimum(chunk + 1, chunks + 1)
+        start = pl.multiple_of(chunk * ROWS, ROWS)
+        tall = 2 * ROWS
+
+        def get(ref, index):
+            return ref[index, pl.ds(start + ROWS, tall), :]
 
         def around(ref, index):
-            here = get(ref, index, chunk)
-            up = jnp.where(
-                row == 0, pltpu.roll(get(ref, index, prev), 1, 0), pltpu.roll(here, 1, 0)
+            window = ref[index, pl.ds(start, tall + 2 * ROWS), :]
+            return (
+                window[ROWS : ROWS + tall],
+                window[ROWS - 1 : ROWS - 1 + tall],
+                window[ROWS + 1 : ROWS + 1 + tall],
             )
-            down = jnp.where(
-                row == ROWS - 1,
-                pltpu.roll(get(ref, index, after), ROWS - 1, 0),
-                pltpu.roll(here, ROWS - 1, 0),
-            )
-            return here, up, down
 
         temp, temp_up, temp_down = around(source, plane % slots)
         cond, cond_up, cond_down = around(conds, plane % cond_slots)
@@ -217,47 +211,43 @@
         net = east - pltpu.roll(east, 1, 1)
         net += (cond + cond_up) * (temp_up - temp) + (cond + cond_down) * (temp_down - temp)
         for other in (upper, lower):
-            other_cond = get(conds, other % cond_slots, chunk)
-            net += (cond + other_cond) * (get(source, other % slots, chunk) - temp)
+            other_cond = get(conds, other % cond_slots)
+            net += (cond + other_cond) * (get(source, other % slots) - temp)
         return temp + (0.5 * STEP_RATE) * net
 
     @pl.when(step < depth_len)
     def _():
-        def place(ref, slot, centre, above, below, before, after):
-            ref[slot, ROWS : ROWS + rows, LANES : LANES + cols] = centre
-            ref[slot, :ROWS, LANES : LANES + cols] = above[0]
-            ref[slot, ROWS + rows :, LANES : LANES + cols] = below[0]
-            ref[slot, :, :LANES] = before[0]
-            ref[slot, :, LANES + cols :] = after[0]
+        def place(ref, slot, centre, above, below, side):
+            ref[slot, 2 * ROWS : 2 * ROWS + rows, :cols] = centre
+            ref[slot, ROWS : 2 * ROWS, :cols] = above[0]
+            ref[slot, 2 * ROWS + rows : 3 * ROWS + rows, :cols] = below[0]
+            ref[slot, ROWS : 3 * ROWS + rows, cols:] = side[0]
 
         phases = jnp.where(phase_ref[0] == 1, cond_ref[1], cond_ref[0])
-        place(temps, step % 3, temp_ref[0], above_t, below_t, before_t, after_t)
-        place(conds, step % 4, phases, above_c, below_c, before_c, after_c)
+        place(temps, step % 3, temp_ref[0], above_t, below_t, side_t)
+        place(conds, step % 4, phases, above_c, below_c, side_c)
 
     @pl.when((step >= 1) & (step <= depth_len))
     def _():
-        @pl.loop(0, chunks + 2)
-        def _(chunk):
-            start = pl.multiple_of(chunk * ROWS, ROWS)
-            nexts[(step - 1) % 3, pl.ds(start, ROWS), :] = conductance_step(
-                step - 1, temps, 3, chunk
+        @pl.loop(0, (chunks + 2) // 2)
+        def _(pair):
+            start = pl.multiple_of(2 * pair * ROWS, ROWS) + ROWS
+            nexts[(step - 1) % 3, pl.ds(start, 2 * ROWS), :] = conductance_step(
+                step - 1, temps, 3, 2 * pair
             )
 
     @pl.when(step >= 2)
     def _():
-        @pl.loop(0, chunks)
-        def _(chunk):
-            start = pl.multiple_of(chunk * ROWS, ROWS)
-            result = conductance_step(step - 2, nexts, 3, chunk + 1)
-            out_ref[0, pl.ds(start, ROWS), :] = result[:, LANES : LANES + cols]
-
-
-def two_steps(solid_temp, phase_map, phase_conductivity, above, below, before, after):
+        @pl.loop(0, chunks // 2)
+        def _(pair):
+            start = pl.multiple_of(2 * pair * ROWS, ROWS)
+            result = conductance_step(step - 2, nexts, 3, 2 * pair + 1)
+            out_ref[0, pl.ds(start, 2 * ROWS), :] = result[:, :cols]
+
+
+def two_steps(solid_temp, phase_map, phase_conductivity, above, below, side):
     depth_len, rows, cols = solid_temp.shape
-    tall, wide = rows + 2 * ROWS, cols + 2 * LANES
-    before = jnp.pad(before, ((0, 0), (0, 0), (LANES - WIDTH, 0)))
-    after = jnp.pad(after, ((0, 0), (0, 0), (0, LANES - WIDTH)))
-
+    tall, wide = rows + 2 * ROWS, cols + LANES
     def spec(*shape, offset=0):
         return pl.BlockSpec(
             (1,) + shape, lambda i: (jnp.minimum(i, depth_len - 1) + offset, 0, 0)
@@ -276,14 +266,13 @@
             *pair(ROWS, cols),
             *pair(ROWS, cols),
             *pair(tall, LANES),
-            *pair(tall, LANES),
         ],
         out_specs=pl.BlockSpec((1, rows, cols), lambda i: (jnp.maximum(i - 2, 0), 0, 0)),
         out_shape=jax.ShapeDtypeStruct((depth_len, rows, cols), jnp.float32),
         scratch_shapes=[
-            pltpu.VMEM((3, tall, wide), jnp.float32),
-            pltpu.VMEM((4, tall, wide), jnp.float32),
-            pltpu.VMEM((3, tall, wide), jnp.float32),
+            pltpu.VMEM((3, tall + 2 * ROWS, wide), jnp.float32),
+            pltpu.VMEM((4, tall + 2 * ROWS, wide), jnp.float32),
+            pltpu.VMEM((3, tall + 2 * ROWS, wide), jnp.float32),
         ],
         compiler_params=params(),
         cost_estimate=pl.CostEstimate(
@@ -294,7 +283,7 @@
         name="conduct_twice",
     )(
         phase_conductivity, solid_temp, phase_map,
-        above, above, below, below, before, before, after, after,
+        above, above, below, below, side, side,
     )
 
 
@@ -352,14 +341,6 @@
         for part in (slice(0, ROWS), slice(tile_rows - ROWS, tile_rows))
     ]
     above, below = swap_edges(jnp.concatenate(edge_rows, axis=1), "grp", 1, ROWS)
-    edge_cols = []
-    for part in (slice(0, WIDTH), slice(stream_loc - WIDTH, stream_loc)):
-        inner = jnp.concatenate(
-            [solid_temp[:, :, part], conductivity(phase_map[:, :, part]), gas_wall_temp[None, :, part]]
-        )
-        edge_cols.append(jnp.concatenate([above[:, :, part], inner, below[:, :, part]], axis=1))
-    before, after = swap_edges(jnp.concatenate(edge_cols, axis=2), "pen", 2, WIDTH)
-
     spectral = pl.pallas_call(
         span_forward_kernel,
         grid=(depth_loc,),
@@ -377,11 +358,20 @@
         ),
         name="span_forward",
     )(pressure_source, table_parts)
-    spectral, above, below, before, after = lax.optimization_barrier(
-        (spectral, above, below, before, after)
-    )
+    spectral, above, below = lax.optimization_barrier((spectral, above, below))
+    moved = lax.all_to_all(spectral, "grp", split_axis=0, concat_axis=0, tiled=True)
+    edge_cols = []
+    for part in (slice(0, WIDTH), slice(stream_loc - WIDTH, stream_loc)):
+        inner = jnp.concatenate(
+            [solid_temp[:, :, part], conductivity(phase_map[:, :, part]), gas_wall_temp[None, :, part]]
+        )
+        edge_cols.append(jnp.concatenate([above[:, :, part], inner, below[:, :, part]], axis=1))
+    before, after = swap_edges(jnp.concatenate(edge_cols, axis=2), "pen", 2, WIDTH)
+    gap = jnp.zeros(before.shape[:2] + (LANES - 2 * WIDTH,), f32)
+    side = jnp.concatenate([after, gap, before], axis=2)
+    moved, side = lax.optimization_barrier((moved, side))
     unheated = two_steps(
-        solid_temp, phase_map, phase_conductivity, above, below, before, after
+        solid_temp, phase_map, phase_conductivity, above, below, side
     )
 
     def top_plane(inner, plane):
@@ -391,7 +381,6 @@
 
     top_cond = top_plane(conductivity(phase_map[0]), solid_len)
     dry_flux = top_plane(gas_wall_temp, 2 * solid_len) - top_plane(solid_temp[0], 0)
-    moved = lax.all_to_all(spectral, "grp", split_axis=0, concat_axis=0, tiled=True)
     moved = moved.reshape(depth_len, stream_loc, waves_loc)
 
     data_spec = pl.BlockSpec((depth_len, stream_loc, LANES), lambda w: (0, 0, w))

time: 487 us -> 385 us (0.79)
  Pallas kernels: 243 us -> 165 us
  waiting for transfers between devices: 99.9 us -> 73.2 us
  other arithmetic: 23.4 us -> 31.5 us
  local copies, waits for them, and re-layouts: 47.3 us -> 42.4 us
    pallas_call x1, Pallas kernels: 174 us -> 96 us  [two_steps(): pl.pallas_call(functools.partial(steps_kernel, depth_len), grid=(depth_le...]
    all_to_all x1, waiting for transfers between devices: 90.1 us -> 45 us  [per_device(): lax.all_to_all(spectral, 'grp', split_axis=0, concat_axis=0, tiled=True)]
    all_gather x1, waiting for transfers between devices: 9.73 us -> 23.6 us  [per_device(): wall_waves = lax.all_gather(solved[0], 'grp')]
    pad x2 -> x0, local copies, waits for them, and re-layouts: 8.29 us -> none  [the longest x1 5.91 us: two_steps(): before = jnp.pad(before, ((0, 0), (0, 0), (LANES - WIDTH, 0)))]
    concatenate x0 -> x1, other arithmetic: none -> 7.15 us  [per_device(): side = jnp.concatenate([after, gap, before], axis=2)]
    optimization_barrier x2 -> x0, local copies, waits for them, and re-layouts: 6.09 us -> none  [per_device(): lax.optimization_barrier((spectral, above, below, before, after))]
    ppermute x0 -> x2, local copies, waits for them, and re-layouts: none -> 6.08 us  [the longest x1 3.05 us: swap_edges(): lax.ppermute(tail, axis, [(i, (i + 1) % count) for i in range(count)])]
  transfers between devices with their start and end apart: 9 -> 9, of which waited for: 2 -> 5; matrix products, arithmetic and copies ran while one was open for 12% -> 17% of each run, Pallas kernels for 38% -> 28%
where the time goes in v4:
time: 385 us; the launch traced here: 384 us
  Pallas kernels  165 us (43%)
  waiting for transfers between devices  73.2 us (19%)
  local copies, waits for them, and re-layouts  42.4 us (11%)
  other arithmetic  31.5 us (8%)
  blocking collectives  31.2 us (8%)
  starting transfers between devices  23.7 us (6%)
  between operations  14.3 us (4%)
    pallas_call x1, Pallas kernels, two_steps(): pl.pallas_call(functools.partial(steps_kernel, depth_len), grid=(depth_le...  96 us
    all_to_all x1, waiting for transfers between devices, per_device(): lax.all_to_all(spectral, 'grp', split_axis=0, concat_axis=0, tiled=True)  45 us
    all_gather x1, blocking collectives, per_device(): gathered = lax.all_gather(jnp.stack([tail_all, head_all]), 'pen')  31.2 us
    pallas_call x1, Pallas kernels, per_device(): pl.pallas_call(lambda s, r, m, h, t: ends_kernel(vectors, s, FirstRow(r),...  24 us
    all_gather x1, waiting for transfers between devices, per_device(): wall_waves = lax.all_gather(solved[0], 'grp')  23.6 us
    pallas_call x1, Pallas kernels, per_device(): pl.pallas_call(lambda m, r, g, a, b, o, c: solve_kernel(vectors, m, First...  21.3 us
    pallas_call x1, Pallas kernels, per_device(): pl.pallas_call(span_forward_kernel, grid=(depth_loc,), in_specs=[pl.Block...  12 us
    pallas_call x1, Pallas kernels, per_device(): pl.pallas_call(span_inverse_kernel, grid=(depth_loc,), in_specs=[pl.Block...  11.6 us
  transfers between devices with their start and end apart: 9, of which 5 were waited for; matrix products, arithmetic and copies ran while one was open for 17% of the time, Pallas kernels for 28%

profile of v4, /device:TPU:0, one launch (start us, length us, event | category | flops | bytes accessed | tf_op | source)
XLA Modules:
  0.0 384.0 jit_solution(1503226912572708268)
XLA Ops:
  9.3 2.7 fusion.23
  12.6 2.0 collective-permute-start.1
  14.6 12.0 %span_forward.1 = f32[4,4,512,256]{3,2,1,0:T(8,128)} custom-call(f32[4,1024,512]{2,1,0:T(8,128)} %source_ref.1, bf16[2,2,512,512]{3,2,1,0:T(8,128)(2,1)} %constant.130.clone.table_ref), custom_call_target="tpu_custom_call" | custom-call | flops 6442450944 | bytes 16777216 | tf_op jit(solution)/shard_map/span_forward/pallas_call | solution.py:344
  27.1 5.7 %all-to-all-start = ((f32[4,4,512,256]{3,2,1,0:T(8,128)}), f32[4,4,512,256]{3,2,1,0:T(8,128)}, u32[]{:S(2)}, u32[]{:S(2)}) async-start(f32[4,4,512,256]{3,2,1,0:T(8,128)} %span_forward.1), calls=%async_computation | async-start | bytes 16777216 | tf_op jit(solution)/shard_map/all_to_all | solution.py:362
  32.8 4.3 %fusion.81 = (s32[16,256,2]{2,1,0:T(8,128)}, s32[16,256,2]{2,1,0:T(8,128)S(1)}) fusion(s32[16,256,512]{2,1,0:T(8,128)} %phase_ref.1), kind=kLoop, calls=%fused_computation.144 | loop fusion | bytes 131072 | tf_op jit(solution)/shard_map/slice | solution.py:366
  37.1 2.2 copy.53
  39.3 4.9 %fusion.80 = (f32[16,256,2]{2,1,0:T(8,128)}, f32[16,256,2]{2,1,0:T(8,128)}) fusion(f32[16,256,512]{2,1,0:T(8,128)} %temp_ref.1), kind=kLoop, calls=%fused_computation.143 | loop fusion | bytes 131072 | tf_op jit(solution)/shard_map/slice | solution.py:366
  44.2 2.2 copy.52
  48.2 2.2 copy.55
  51.6 1.5 dynamic-slice_bitcast_fusion.4
  57.8 4.8 %collective-permute-start.2 = (f32[33,272,2]{1,2,0:T(2,128)S(1)}, f32[33,272,2]{1,2,0:T(2,128)S(1)}, u32[]{:S(2)}, u32[]{:S(2)}) collective-permute-start(f32[33,272,2]{1,2,0:T(2,128)S(1)} %pad_maximum_fusion.3), channel_id=1, source_target_pairs={{1,0},{2,1},{3,2},{4,3},{5,4},{6,5},{7,6},{0,7},{9,8},{10,9},{11,1... | collective-permute-start | bytes 215432 | tf_op jit(solution)/shard_map/ppermute | solution.py:33
  65.4 3.0 copy.42
  68.4 2.7 collective-permute-done.3
  71.1 3.0 copy.43
  74.1 7.1 %pad_maximum_fusion.side_t.side_c = f32[33,272,128]{2,1,0:T(8,128)} fusion(f32[33,272,2]{2,1,0:T(8,128)} %copy.43, f32[33,272,2]{2,1,0:T(8,128)} %copy.42, f32[128]{0:T(128)S(1)} %pad.33.clone), kind=kLoop, calls=%fused_computation | loop fusion | flops 2297856 | bytes 4739840 | tf_op jit(solution)/shard_map/concatenate | solution.py:371
  81.3 45.0 %all-to-all-done = f32[4,4,512,256]{3,2,1,0:T(8,128)} async-done(((f32[4,4,512,256]{3,2,1,0:T(8,128)}), f32[4,4,512,256]{3,2,1,0:T(8,128)}, u32[]{:S(2)}, u32[]{:S(2)}) %all-to-all-start) | async-done | bytes 8388640 | tf_op jit(solution)/shard_map/all_to_all | solution.py:362
  126.3 24.0 %stream_ends.1 = (f32[16,64,8,256]{3,2,1,0:T(8,128)}, f32[16,8,256]{2,1,0:T(8,128)}, f32[16,8,256]{2,1,0:T(8,128)}) custom-call(f32[16,512,256]{2,1,0:T(8,128)} %bitcast.6.s, f32[16,1,256]{2,1,0:T(1,128)} %get-tuple-element.104.r), custom_call_target="tpu_custom_call" | custom-call | flops 67108864 | bytes 16777216 | tf_op jit(solution)/shard_map/stream_ends/pallas_call | solution.py:400
  150.3 2.4 fusion.63
  152.7 31.2 %all-gather = f32[16,16,256]{2,1,0:T(8,128)S(1)} all-gather(f32[2,16,256]{2,1,0:T(8,128)S(1)} %copy.44), channel_id=2, replica_groups=mesh['grp'=4,'pen'=8] {'pen'}, dimensions={0}, use_global_device_ids=true | all-gather | bytes 294912 | tf_op jit(solution)/shard_map/all_gather | solution.py:419
  184.1 2.2 fusion.59
  187.9 21.3 %stream_solve.1 = f32[16,512,256]{2,1,0:T(8,128)} custom-call(f32[16,64,8,256]{3,2,1,0:T(8,128)} %get-tuple-element.38.m, f32[16,1,256]{2,1,0:T(1,128)} %get-tuple-element.104.r, f32[16,1,256]{2,1,0:T(1,128)} %get-tuple-element.103.g, f32[16,8,256]{2,1,0:T(8,128)} %stack.10.a, f32[16,8,256]{2,1,0:T(8,128)} %stack.11.b), custom_call_target="tpu_custom_call" | custom-call | flops 67108864 | bytes 16777216 | tf_op jit(solution)/shard_map/stream_solve/pallas_call | solution.py:425
  209.3 5.7 %all-to-all-start.1 = ((f32[4,4,512,256]{3,2,1,0:T(8,128)}), f32[4,4,512,256]{3,2,1,0:T(8,128)}, u32[]{:S(2)}, u32[]{:S(2)}) async-start(f32[4,4,512,256]{3,2,1,0:T(8,128)} %bitcast.222), calls=%async_computation.1 | async-start | bytes 16777216 | tf_op jit(solution)/shard_map/all_to_all | solution.py:437
  215.2 1.9 slice.357
  220.1 3.3 select_bitcast_fusion
  229.5 23.6 %all-gather.3.cloned.1.call-done = f32[4,512,256]{2,1,0:T(8,128)} async-done(((f32[1,512,256]{2,1,0:T(8,128)}), f32[4,512,256]{2,1,0:T(8,128)}) %all-gather.3.cloned.1.call-update) | async-done | bytes 2097168 | tf_op jit(solution)/shard_map/all_gather | solution.py:467
  253.1 2.7 fusion
  255.9 1.5 collective-permute-start.4
  257.4 3.2 collective-permute-start.5
  260.7 96.0 %conduct_twice.1 = f32[16,256,512]{2,1,0:T(8,128)} custom-call(f32[2]{0:T(128)} %cond_ref.1, f32[16,256,512]{2,1,0:T(8,128)} %temp_ref.1, s32[16,256,512]{2,1,0:T(8,128)} %phase_ref.1, f32[33,8,512]{2,1,0:T(8,128)} %copy-done, f32[33,8,512]{2,1,0:T(8,128)} %copy-done, f32[33,8,512]{2,1,0:T(8,128)} %copy-done.1, f32[33,8,512]{2,1,0:T(8,128)} %copy-done.1, ...), custom_call_target="tpu_custom_call" | custom-call | flops 125829120 | bytes 33554432 | tf_op jit(solution)/shard_map/conduct_twice/pallas_call | solution.py:259
  357.4 4.6 %fusion.8 = f32[16,256,512]{2,1,0:T(8,128)} fusion(f32[16,256,512]{2,1,0:T(8,128)} %conduct_twice.1, f32[1,258,514]{2,1,0:T(8,128)S(1)} %fusion.2, f32[1,258,514]{2,1,0:T(8,128)S(1)} %maximum_bitcast_fusion, s32[16,256,512]{2,1,0:T(8,128)} %phase_ref.1, pred[1,256,512]{2,1,0:T(8,128)(4,1)S(1)} %get-tuple-element.45, f32[]{:T(128)} %bitcast.1, f32[]{:T(128)} %bitcast), kind=kLoop, calls=%fused_computation.19 | loop fusion | flops 4194304 | bytes 6947840 | tf_op jit(solution)/shard_map/scatter-add | solution.py:483
  362.0 3.6 fusion.9
  365.6 11.6 %span_inverse.1 = f32[4,1024,512]{2,1,0:T(8,128)} custom-call(f32[4,4,512,256]{3,2,1,0:T(8,128)} %all-to-all-done.1.waves_ref, bf16[2,2,512,512]{3,2,1,0:T(8,128)(2,1)} %constant.130.clone.table_ref), custom_call_target="tpu_custom_call" | custom-call | flops 6442450944 | bytes 16777216 | tf_op jit(solution)/shard_map/span_inverse/pallas_call | solution.py:444
  (71 shorter events, 25.4 us)
Async XLA Ops:
  12.0 14.6 %collective-permute-start = (f32[33,8,512]{2,1,0:T(8,128)S(1)}, f32[33,8,512]{2,1,0:T(8,128)S(1)}, u32[]{:S(2)}, u32[]{:S(2)}) collective-permute-start(f32[33,8,512]{2,1,0:T(8,128)S(1)} %pad_maximum_fusion.1), channel_id=1, source_target_pairs={{0,8},{8,16},{16,24},{24,0},{1,9},{9,17},{17,25},{25,1},{2,10},{10... | collective-permute-start | bytes 1622024 | tf_op jit(solution)/shard_map/ppermute | solution.py:32
  12.6 14.6 %collective-permute-start.1 = (f32[33,8,512]{2,1,0:T(8,128)S(1)}, f32[33,8,512]{2,1,0:T(8,128)S(1)}, u32[]{:S(2)}, u32[]{:S(2)}) collective-permute-start(f32[33,8,512]{2,1,0:T(8,128)S(1)} %pad_maximum_fusion.2), channel_id=1, source_target_pairs={{8,0},{16,8},{24,16},{0,24},{9,1},{17,9},{25,17},{1,25},{10,2},{18... | collective-permute-start | bytes 1622024 | tf_op jit(solution)/shard_map/ppermute | solution.py:33
  26.6 196.8 %copy-start = (f32[33,8,512]{2,1,0:T(8,128)}, f32[33,8,512]{2,1,0:T(8,128)S(1)}, u32[]{:S(2)}) copy-start(f32[33,8,512]{2,1,0:T(8,128)S(1)} %collective-permute-done.above_t.above_c) | copy-start | bytes 1622020
  27.1 30.0 %copy-start.1 = (f32[33,8,512]{2,1,0:T(8,128)}, f32[33,8,512]{2,1,0:T(8,128)S(1)}, u32[]{:S(2)}) copy-start(f32[33,8,512]{2,1,0:T(8,128)S(1)} %collective-permute-done.1.below_t.below_c) | copy-start | bytes 1622020
  27.1 99.2 %all-to-all-start = ((f32[4,4,512,256]{3,2,1,0:T(8,128)}), f32[4,4,512,256]{3,2,1,0:T(8,128)}, u32[]{:S(2)}, u32[]{:S(2)}) async-start(f32[4,4,512,256]{3,2,1,0:T(8,128)} %span_forward.1), calls=%async_computation | async-start | bytes 16777216 | tf_op jit(solution)/shard_map/all_to_all | solution.py:362
  57.8 7.6 %collective-permute-start.2 = (f32[33,272,2]{1,2,0:T(2,128)S(1)}, f32[33,272,2]{1,2,0:T(2,128)S(1)}, u32[]{:S(2)}, u32[]{:S(2)}) collective-permute-start(f32[33,272,2]{1,2,0:T(2,128)S(1)} %pad_maximum_fusion.3), channel_id=1, source_target_pairs={{1,0},{2,1},{3,2},{4,3},{5,4},{6,5},{7,6},{0,7},{9,8},{10,9},{11,1... | collective-permute-start | bytes 215432 | tf_op jit(solution)/shard_map/ppermute | solution.py:33
  63.3 7.8 %collective-permute-start.3 = (f32[33,272,2]{1,2,0:T(2,128)S(1)}, f32[33,272,2]{1,2,0:T(2,128)S(1)}, u32[]{:S(2)}, u32[]{:S(2)}) collective-permute-start(f32[33,272,2]{1,2,0:T(2,128)S(1)} %pad_maximum_fusion.4), channel_id=1, source_target_pairs={{0,1},{1,2},{2,3},{3,4},{4,5},{5,6},{6,7},{7,0},{8,9},{9,10},{10,1... | collective-permute-start | bytes 215432 | tf_op jit(solution)/shard_map/ppermute | solution.py:32
  65.4 8.8 %copy-start.3 = (f32[33,272,2]{1,2,0:T(2,128)}, f32[33,272,2]{1,2,0:T(2,128)S(1)}, u32[]{:S(2)}) copy-start(f32[33,272,2]{1,2,0:T(2,128)S(1)} %collective-permute-done.2) | copy-start | bytes 215428
  71.1 10.2 %copy-start.4 = (f32[33,272,2]{1,2,0:T(2,128)}, f32[33,272,2]{1,2,0:T(2,128)S(1)}, u32[]{:S(2)}) copy-start(f32[33,272,2]{1,2,0:T(2,128)S(1)} %collective-permute-done.3) | copy-start | bytes 215428
  81.3 69.0 %copy-start.5 = (f32[4,16,256]{2,0,1:T(4,128)S(1)}, f32[4,16,256]{2,0,1:T(4,128)}, u32[]{:S(2)}) copy-start(f32[4,16,256]{2,0,1:T(4,128)} %constant.133.clone) | copy-start | bytes 196612
  209.3 156.3 %all-to-all-start.1 = ((f32[4,4,512,256]{3,2,1,0:T(8,128)}), f32[4,4,512,256]{3,2,1,0:T(8,128)}, u32[]{:S(2)}, u32[]{:S(2)}) async-start(f32[4,4,512,256]{3,2,1,0:T(8,128)} %bitcast.222), calls=%async_computation.1 | async-start | bytes 16777216 | tf_op jit(solution)/shard_map/all_to_all | solution.py:437
  215.0 9.2 %copy-start.2 = (f32[256,512]{1,0:T(8,128)S(1)}, f32[256,512]{1,0:T(8,128)}, u32[]{:S(2)}) copy-start(f32[256,512]{1,0:T(8,128)} %param.17) | copy-start | bytes 1572868
  215.0 38.1 %all-gather.3.cloned.1.call-start = ((), (), s32[]{:S(2)}) async-start(), calls=%async_computation.2 | async-start | bytes 2621440 | tf_op jit(solution)/shard_map/all_gather | solution.py:467
  255.9 100.8 %collective-permute-start.4 = (f32[258,1]{1,0:T(8,128)S(1)}, f32[258,1]{1,0:T(8,128)S(1)}, u32[]{:S(2)}, u32[]{:S(2)}) collective-permute-start(f32[258,1]{1,0:T(8,128)S(1)} %get-tuple-element.74), channel_id=1, source_target_pairs={{0,1},{1,2},{2,3},{3,4},{4,5},{5,6},{6,7},{7,0},{8,9},{9,10},{10,1... | collective-permute-start | bytes 3104 | tf_op jit(solution)/shard_map/ppermute | solution.py:32
  257.4 99.3 %collective-permute-start.5 = (f32[258,1]{1,0:T(8,128)S(1)}, f32[258,1]{1,0:T(8,128)S(1)}, u32[]{:S(2)}, u32[]{:S(2)}) collective-permute-start(f32[258,1]{1,0:T(8,128)S(1)} %get-tuple-element.75), channel_id=1, source_target_pairs={{1,0},{2,1},{3,2},{4,3},{5,4},{6,5},{7,6},{0,7},{9,8},{10,9},{11,1... | collective-permute-start | bytes 3104 | tf_op jit(solution)/shard_map/ppermute | solution.py:33
Sparse Core Ops, SparseCore 0:
  217.9 35.1 all-gather.2
